TPU v7x, 512 devices: a whole 4x4x16 slice. The times are simulated.
512 devices in a mesh: rep: 8 (over z_hi, core), ep: 64 (over x, y, z_lo).
Axes of the slice: x: 4, y: 4, z: 16 (z_hi: 4, z_lo: 4; z = z_hi * 4 + z_lo), core: 2. Of those that a mesh axis runs over, the one named last changes fastest.
Arguments:
- rows_old: bfloat16 [2048, 3584], P('ep'), may hold values from -6 to 6
- rows_new: bfloat16 [2048, 3584], P('ep'), may hold values from -6 to 6
- routes_old: int32 [2048, 8], P('ep'), may hold values from 0 to 63, all different within a row; in each aligned block of 32 rows (0 to 31, 32 to 63, ...) at most 6 rows name the same one
- routes_new: int32 [2048, 8], P('ep'), may hold values from 0 to 63, all different within a row; in each aligned block of 32 rows (0 to 31, 32 to 63, ...) at most 6 rows name the same one
- gates_old: float32 [2048, 8], P('ep'), may hold values from 0.05 to 0.5
- gates_new: float32 [2048, 8], P('ep'), may hold values from 0.05 to 0.5
- w_in_old: bfloat16 [64, 3584, 2, 1024], P('ep', None, None, 'rep'), may hold values from -0.09375 to 0.09375
- w_in_new: bfloat16 [64, 3584, 2, 1024], P('ep', 'rep'), may hold values from -0.09375 to 0.09375
- w_out: bfloat16 [64, 1024, 3584], P('ep', 'rep'), may hold values from -0.1875 to 0.1875
Outputs:
- out_old: bfloat16 [2048, 3584], P('ep', 'rep')
- out_new: bfloat16 [2048, 3584], P('ep', 'rep')
Inputs may be any that keep to these rules, and one draw needn't show every extreme that they name: `routes_old`: each row names 8 different experts; within the 32 rows of one device no expert is named more than 6 times. `routes_new`: each row names 8 different experts; within the 32 rows of one device no expert is named more than 6 times.
All inputs are finite; a program needn't handle non-finite values.
Results may differ from a plain program's by a relative error of at most 0.02.
Values may be sent and summed in bfloat16 or wider, within the bound.
A program may use at most 64 MiB of HBM per device.

v0:
```python
import jax
import jax.numpy as jnp
from jax import lax
from jax.sharding import PartitionSpec as P


def slot_table(routing, capacity, count):
    flattened = routing.reshape(-1)
    onehot = (flattened[:, None] == jnp.arange(count, dtype=jnp.int32)[None, :]).astype(jnp.int32)
    before = jnp.cumsum(onehot, axis=0) - onehot
    slot_rank = jnp.sum(before * onehot, axis=1)
    return flattened * capacity + slot_rank


def source_rows(positions, topk, capacity, count):
    pair_index = jnp.arange(positions.shape[0], dtype=jnp.int32)
    sources = jnp.zeros((count * capacity,), jnp.int32).at[positions].set(pair_index // topk)
    filled = jnp.zeros((count * capacity,), jnp.int32).at[positions].set(1)
    return (sources, filled)


def body(
    rows_old, rows_new, routes_old, routes_new, gates_old, gates_new, w_in_old, w_in_new, w_out
):
    experts = lax.axis_size("ep")
    rows_count, width = rows_old.shape
    topk = routes_old.shape[1]
    capacity = 3 * rows_count * topk // (2 * experts)
    resident = w_in_old[0]
    down = w_out[0]

    def run_batch(tokens, routing, gates, weights):
        positions = slot_table(routing, capacity, experts)
        sources, filled = source_rows(positions, topk, capacity, experts)
        send = tokens[sources] * filled[:, None].astype(tokens.dtype)
        send = send.reshape(experts, capacity, width)
        full_in = lax.all_to_all(send, "ep", split_axis=0, concat_axis=0, tiled=True)
        act = jnp.einsum("ecd,dgh->ecgh", full_in, weights, preferred_element_type=jnp.float32)
        hidden = (jax.nn.silu(act[:, :, 0]) * act[:, :, 1]).astype(jnp.bfloat16)
        partial_value = jnp.einsum(
            "ech,hd->ecd", hidden, down, preferred_element_type=jnp.float32
        ).astype(jnp.bfloat16)
        back = lax.all_to_all(partial_value, "ep", split_axis=0, concat_axis=0, tiled=True)
        values = back.reshape(experts * capacity, width)[positions].reshape(rows_count, topk, width)
        combined = jnp.einsum("rk,rkd->rd", gates, values.astype(jnp.float32))
        return lax.psum_scatter(
            combined.astype(jnp.bfloat16), "rep", scatter_dimension=1, tiled=True
        )

    refreshed_weights = lax.all_to_all(w_in_new, "rep", split_axis=3, concat_axis=1, tiled=True)[0]
    out_old = run_batch(rows_old, routes_old, gates_old, resident)
    out_new = run_batch(rows_new, routes_new, gates_new, refreshed_weights)
    return (out_old, out_new)


def solution(mesh):
    return jax.shard_map(
        body,
        mesh=mesh,
        in_specs=(
            P("ep", None),
            P("ep", None),
            P("ep", None),
            P("ep", None),
            P("ep", None),
            P("ep", None),
            P("ep", None, None, "rep"),
            P("ep", "rep", None, None),
            P("ep", "rep", None),
        ),
        out_specs=(P("ep", "rep"), P("ep", "rep")),
        check_vma=False,
    )
```

profile of v0, /device:TPU:7, one launch (start us, length us, event | category | flops | bytes accessed | tf_op | source)
XLA Modules:
  0.0 575.2 jit_solution(18040079837875007895)
XLA Ops:
  7.2 8.7 %copy.55 = bf16[1,448,2,1024]{1,2,0,3:T(2,128)(2,1)} copy(bf16[1,448,2,1024]{3,2,1,0:T(2,128)(2,1)} %param.16) | data formatting | bytes 3670016 | tf_op args[7]
  15.8 15.9 %all-to-all-start.3 = ((bf16[1,448,2,1024]{1,2,0,3:T(2,128)(2,1)}), bf16[1,448,2,1024]{1,2,0,3:T(2,128)(2,1)S(1)}, u32[]{:S(2)}, u32[]{:S(2)}) async-start(bf16[1,448,2,1024]{1,2,0,3:T(2,128)(2,1)} %copy.55), calls=%async_computation.3 | async-start | bytes 4194304 | tf_op jit(solution)/shard_map/all_to_all | solution.py:50
  32.0 0.6 reduce-window.16
  32.6 0.2 slice_reduce_fusion
  33.0 0.1 fusion.20
  33.1 1.4 scatter_custom_fusion.2
  34.6 3.9 gather_fusion.2
  38.5 5.4 gather.20
  43.9 1.4 scatter_custom_fusion.3
  45.3 0.1 mul.82
  45.4 4.2 broadcast_multiply_fusion
  49.6 72.5 %all-to-all-done.3 = bf16[1,448,2,1024]{1,2,0,3:T(2,128)(2,1)S(1)} async-done(((bf16[1,448,2,1024]{1,2,0,3:T(2,128)(2,1)}), bf16[1,448,2,1024]{1,2,0,3:T(2,128)(2,1)S(1)}, u32[]{:S(2)}, u32[]{:S(2)}) %all-to-all-start.3) | async-done | bytes 1835040 | tf_op jit(solution)/shard_map/all_to_all | solution.py:50
  122.1 13.9 %all-to-all-start.2 = ((bf16[64,6,3584]{2,1,0:T(8,128)(2,1)}), bf16[64,6,3584]{2,1,0:T(8,128)(2,1)}, u32[]{:S(2)}, u32[]{:S(2)}) async-start(bf16[64,6,3584]{2,1,0:T(8,128)(2,1)} %broadcast_multiply_fusion), calls=%async_computation.2 | async-start | bytes 7340032 | tf_op jit(solution)/shard_map/all_to_all | solution.py:37
  136.3 0.6 reduce-window.14
  136.9 0.2 slice_reduce_fusion.1
  137.4 0.1 fusion.23
  137.5 1.4 scatter_custom_fusion
  138.9 1.4 scatter_custom_fusion.1
  140.3 3.9 gather_fusion
  144.2 5.5 gather.17
  149.7 0.1 mul.74
  149.9 4.3 broadcast_multiply_fusion.1
  154.1 62.5 %all-to-all-done.2 = bf16[64,6,3584]{2,1,0:T(8,128)(2,1)} async-done(((bf16[64,6,3584]{2,1,0:T(8,128)(2,1)}), bf16[64,6,3584]{2,1,0:T(8,128)(2,1)}, u32[]{:S(2)}, u32[]{:S(2)}) %all-to-all-start.2) | async-done | bytes 2752544 | tf_op jit(solution)/shard_map/all_to_all | solution.py:37
  216.6 7.5 %all-to-all-start = ((bf16[64,6,3584]{2,1,0:T(8,128)(2,1)}), bf16[64,6,3584]{2,1,0:T(8,128)(2,1)}, u32[]{:S(2)}, u32[]{:S(2)}) async-start(bf16[64,6,3584]{2,1,0:T(8,128)(2,1)} %broadcast_multiply_fusion.1), calls=%async_computation | async-start | bytes 7340032 | tf_op jit(solution)/shard_map/all_to_all | solution.py:37
  224.2 3.7 copy.56
  227.9 3.6 fusion
  231.5 0.9 convolution_convert_fusion
  232.4 3.3 copy.58
  235.7 70.0 %all-to-all-done = bf16[64,6,3584]{2,1,0:T(8,128)(2,1)} async-done(((bf16[64,6,3584]{2,1,0:T(8,128)(2,1)}), bf16[64,6,3584]{2,1,0:T(8,128)(2,1)}, u32[]{:S(2)}, u32[]{:S(2)}) %all-to-all-start) | async-done | bytes 2752544 | tf_op jit(solution)/shard_map/all_to_all | solution.py:37
  305.7 7.5 %all-to-all-start.4 = ((bf16[64,6,3584]{2,1,0:T(8,128)(2,1)}), bf16[64,6,3584]{2,1,0:T(8,128)(2,1)}, u32[]{:S(2)}, u32[]{:S(2)}) async-start(bf16[64,6,3584]{2,1,0:T(8,128)(2,1)} %copy.58), calls=%async_computation.4 | async-start | bytes 7340032 | tf_op jit(solution)/shard_map/all_to_all | solution.py:43
  313.2 3.0 fusion.2
  316.3 0.9 convolution_convert_fusion.1
  317.1 3.4 copy.50
  320.5 74.3 %all-to-all-done.4 = bf16[64,6,3584]{2,1,0:T(8,128)(2,1)} async-done(((bf16[64,6,3584]{2,1,0:T(8,128)(2,1)}), bf16[64,6,3584]{2,1,0:T(8,128)(2,1)}, u32[]{:S(2)}, u32[]{:S(2)}) %all-to-all-start.4) | async-done | bytes 2752544 | tf_op jit(solution)/shard_map/all_to_all | solution.py:43
  394.8 7.5 %all-to-all-start.1 = ((bf16[64,6,3584]{2,1,0:T(8,128)(2,1)}), bf16[64,6,3584]{2,1,0:T(8,128)(2,1)}, u32[]{:S(2)}, u32[]{:S(2)}) async-start(bf16[64,6,3584]{2,1,0:T(8,128)(2,1)} %copy.50), calls=%async_computation.1 | async-start | bytes 7340032 | tf_op jit(solution)/shard_map/all_to_all | solution.py:43
  402.3 0.3 reduce-scatter.9.cloned.1.call-start
  402.7 5.5 reshape.133
  408.2 5.7 gather_fusion.3
  413.9 0.6 fusion.4
  414.6 1.2 copy.71
  416.0 85.1 %all-to-all-done.1 = bf16[64,6,3584]{2,1,0:T(8,128)(2,1)} async-done(((bf16[64,6,3584]{2,1,0:T(8,128)(2,1)}), bf16[64,6,3584]{2,1,0:T(8,128)(2,1)}, u32[]{:S(2)}, u32[]{:S(2)}) %all-to-all-start.1) | async-done | bytes 2752544 | tf_op jit(solution)/shard_map/all_to_all | solution.py:43
  501.1 5.5 reshape.130
  506.6 5.7 gather_fusion.1
  512.3 0.6 fusion.6
  512.9 1.2 copy.69
  514.2 1.6 copy.72
  515.8 50.9 %reduce-scatter.7.cloned.1.call-done = bf16[448,32]{1,0:T(8,128)(2,1)} async-done(((bf16[3584,32]{1,0:T(8,128)(2,1)}), bf16[448,32]{1,0:T(8,128)(2,1)}) %reduce-scatter.7.cloned.1.call-update) | async-done | bytes 28688
  566.8 1.6 copy.70
  (54 shorter events, 1.4 us)
Async XLA Ops:
  7.2 224.3 %copy-start = (bf16[1,128,3584]{2,1,0:T(8,128)(2,1)S(1)}, bf16[1,128,3584]{2,1,0:T(8,128)(2,1)}, u32[]{:S(2)}) copy-start(bf16[1,128,3584]{2,1,0:T(8,128)(2,1)} %param.17) | copy-start | bytes 2752516
  15.8 15.9 %copy-start.3 = (s32[32,8]{0,1:T(8,128)S(1)}, s32[32,8]{0,1:T(8,128)}, u32[]{:S(2)}) copy-start(s32[32,8]{0,1:T(8,128)} %param.12) | copy-start | bytes 3076
  15.8 18.7 %copy-start.1 = (bf16[32,3584]{1,0:T(8,128)(2,1)S(1)}, bf16[32,3584]{1,0:T(8,128)(2,1)}, u32[]{:S(2)}) copy-start(bf16[32,3584]{1,0:T(8,128)(2,1)} %param.10) | copy-start | bytes 688132
  15.8 106.3 %all-to-all-start.3 = ((bf16[1,448,2,1024]{1,2,0,3:T(2,128)(2,1)}), bf16[1,448,2,1024]{1,2,0,3:T(2,128)(2,1)S(1)}, u32[]{:S(2)}, u32[]{:S(2)}) async-start(bf16[1,448,2,1024]{1,2,0,3:T(2,128)(2,1)} %copy.55), calls=%async_computation.3 | async-start | bytes 4194304 | tf_op jit(solution)/shard_map/all_to_all | solution.py:50
  49.6 86.4 %copy-start.4 = (s32[32,8]{0,1:T(8,128)S(1)}, s32[32,8]{0,1:T(8,128)}, u32[]{:S(2)}) copy-start(s32[32,8]{0,1:T(8,128)} %param.11) | copy-start | bytes 3076
  49.6 90.7 %copy-start.2 = (bf16[32,3584]{1,0:T(8,128)(2,1)S(1)}, bf16[32,3584]{1,0:T(8,128)(2,1)}, u32[]{:S(2)}) copy-start(bf16[32,3584]{1,0:T(8,128)(2,1)} %param.9) | copy-start | bytes 688132
  122.1 94.5 %all-to-all-start.2 = ((bf16[64,6,3584]{2,1,0:T(8,128)(2,1)}), bf16[64,6,3584]{2,1,0:T(8,128)(2,1)}, u32[]{:S(2)}, u32[]{:S(2)}) async-start(bf16[64,6,3584]{2,1,0:T(8,128)(2,1)} %broadcast_multiply_fusion), calls=%async_computation.2 | async-start | bytes 7340032 | tf_op jit(solution)/shard_map/all_to_all | solution.py:37
  216.6 89.0 %all-to-all-start = ((bf16[64,6,3584]{2,1,0:T(8,128)(2,1)}), bf16[64,6,3584]{2,1,0:T(8,128)(2,1)}, u32[]{:S(2)}, u32[]{:S(2)}) async-start(bf16[64,6,3584]{2,1,0:T(8,128)(2,1)} %broadcast_multiply_fusion.1), calls=%async_computation | async-start | bytes 7340032 | tf_op jit(solution)/shard_map/all_to_all | solution.py:37
  235.7 77.5 %copy-start.7 = (bf16[1,3584,2,128]{3,2,1,0:T(2,128)(2,1)S(1)}, bf16[1,3584,2,128]{3,2,1,0:T(2,128)(2,1)}, u32[]{:S(2)}) copy-start(bf16[1,3584,2,128]{3,2,1,0:T(2,128)(2,1)} %param.15) | copy-start | bytes 5505028
  305.7 89.1 %all-to-all-start.4 = ((bf16[64,6,3584]{2,1,0:T(8,128)(2,1)}), bf16[64,6,3584]{2,1,0:T(8,128)(2,1)}, u32[]{:S(2)}, u32[]{:S(2)}) async-start(bf16[64,6,3584]{2,1,0:T(8,128)(2,1)} %copy.58), calls=%async_computation.4 | async-start | bytes 7340032 | tf_op jit(solution)/shard_map/all_to_all | solution.py:43
  320.5 82.1 %copy-start.5 = (f32[32,8]{0,1:T(8,128)S(1)}, f32[32,8]{0,1:T(8,128)}, u32[]{:S(2)}) copy-start(f32[32,8]{0,1:T(8,128)} %param.14) | copy-start | bytes 3076
  394.8 106.3 %all-to-all-start.1 = ((bf16[64,6,3584]{2,1,0:T(8,128)(2,1)}), bf16[64,6,3584]{2,1,0:T(8,128)(2,1)}, u32[]{:S(2)}, u32[]{:S(2)}) async-start(bf16[64,6,3584]{2,1,0:T(8,128)(2,1)} %copy.50), calls=%async_computation.1 | async-start | bytes 7340032 | tf_op jit(solution)/shard_map/all_to_all | solution.py:43
  402.3 111.9 %reduce-scatter.9.cloned.1.call-start = ((), (), s32[]{:S(2)}) async-start(), calls=%async_computation.8 | async-start | bytes 1032192
  413.9 2.0 copy-start.6
  415.8 151.0 %reduce-scatter.7.cloned.1.call-start = ((), (), s32[]{:S(2)}) async-start(), calls=%async_computation.7 | async-start | bytes 1032192
Sparse Core Ops, SparseCore 0:
  415.9 56.1 reduce-scatter.8
  514.3 52.3 reduce-scatter.6
where the time goes:
time: 577 us; the launch traced here: 575 us
  waiting for transfers between devices  415 us (72%)
  local copies, waits for them, and re-layouts  73.1 us (13%)
  starting transfers between devices  52.6 us (9%)
  between operations  14.4 us (2%)
  other arithmetic  10 us (2%)
  matrix products  9.6 us (2%)
    all_to_all x2, waiting for transfers between devices, run_batch(): lax.all_to_all(partial_value, 'ep', split_axis=0, concat_axis=0, tiled=True)  159 us
    all_to_all x2, waiting for transfers between devices, run_batch(): lax.all_to_all(send, 'ep', split_axis=0, concat_axis=0, tiled=True)  132 us
    all_to_all x1, waiting for transfers between devices, body(): lax.all_to_all(w_in_new, 'rep', split_axis=3, concat_axis=1, tiled=True)[0]  72.5 us
    unnamed x4, waiting for transfers between devices  51 us
    all_to_all x2, starting transfers between devices, run_batch(): lax.all_to_all(send, 'ep', split_axis=0, concat_axis=0, tiled=True)  21.5 us
    gather x4, local copies, waits for them, and re-layouts, run_batch(): send = tokens[sources] * filled[:, None].astype(tokens.dtype)  18.7 us
    all_to_all x1, starting transfers between devices, body(): lax.all_to_all(w_in_new, 'rep', split_axis=3, concat_axis=1, tiled=True)[0]  15.9 us
    all_to_all x2, starting transfers between devices, run_batch(): lax.all_to_all(partial_value, 'ep', split_axis=0, concat_axis=0, tiled=True)  15 us
  transfers between devices with their start and end apart: 7, of which 6 were waited for; matrix products, arithmetic and copies ran while one was open for 14% of the time, Pallas kernels for 0%

commit v1 on v0

v1 whole, which is shorter than its diff:
```python
import functools

import jax
import jax.numpy as jnp
from jax import lax
from jax.experimental import pallas as pl
from jax.experimental.pallas import tpu as pltpu
from jax.sharding import PartitionSpec as P

BF = jnp.bfloat16
F32 = jnp.float32
MESH = pl.DeviceIdType.MESH

D = 3584
HALF = D // 2
BLK = HALF // 2
WIN = 512
SLICE = 448
SLAB = 128
TOPK = 8
ROWS = 32
CAP = 6
SLOTS = 4 * CAP
CH = 4 * SLOTS
ORDER = (2, 1, 3, 0)
ZOFF = (1, 15, 2)


def dot(a, b):
    return lax.dot_general(a, b, (((1,), (0,)), ((), ())), preferred_element_type=F32)


def dot_nt(a, b):
    return lax.dot_general(a, b, (((1,), (1,)), ((), ())), preferred_element_type=F32)


def iota(shape, dim):
    return lax.broadcasted_iota(jnp.int32, shape, dim)


def by24(q):
    return (q * 2731) >> 16


def by6(q):
    return (q * 10923) >> 16


def kernel(
    meta, rows_old, rows_new, w_old, w_new, w_out,
    out_old, out_new,
    meta_z, rz_old, rz_new, disp, comb,
    send_new, recv_new, send_old, recv_old, sib_old,
    pn_own, sx_send, sx_recv, rs_send, rs_recv,
    po, so_send, so_recv, ret_send, ret_recv,
    z1_own, z1_send, z1_recv, z2_send, z2_recv,
    zs, zr, xs, xr, fs, fr, sxs, sxr, rss, rsr, sos, sor, rts, rtr, z1s, z1r, z2s, z2r,
):
    ep = lax.axis_index("ep")
    rep = lax.axis_index("rep")
    core, zh = lax.rem(rep, 2), rep // 2
    zl, me = lax.rem(ep, 4), ep // 4
    x, y = me // 4, lax.rem(me, 4)
    z = zh * 4 + zl

    def z_dev(offset):
        t = lax.rem(z + offset, 16)
        return {"rep": (t // 4) * 2 + core, "ep": me * 4 + lax.rem(t, 4)}

    def peer(dx, dy):
        return lax.rem(x + dx, 4) * 4 + lax.rem(y + dy, 4)

    def xy_dev(d):
        return {"rep": rep, "ep": d * 4 + zl}

    def zh_dev(k):
        return {"rep": lax.rem(zh + k, 4) * 2 + core, "ep": ep}

    sibling = {"rep": zh * 2 + (1 - core), "ep": ep}

    def remote(src, dst, ss, rs, dev):
        return pltpu.make_async_remote_copy(
            src_ref=src, dst_ref=dst, send_sem=ss, recv_sem=rs, device_id=dev, device_id_type=MESH
        )

    barrier = pltpu.get_barrier_semaphore()
    for i in range(1, 16):
        pl.semaphore_signal(barrier, 1, device_id=xy_dev(peer(i // 4, i % 4)), device_id_type=MESH)
    for o in (1, 15, 2, 14):
        pl.semaphore_signal(barrier, 1, device_id=z_dev(o), device_id_type=MESH)
    for k in range(1, 8):
        pl.semaphore_signal(
            barrier, 1, device_id={"rep": lax.rem(rep + k, 8), "ep": ep}, device_id_type=MESH
        )
    half = pl.multiple_of(core * HALF, 128)
    other = pl.multiple_of((1 - core) * HALF, 128)
    mine = pl.ds(pl.multiple_of(zl * ROWS, ROWS), ROWS)
    meta_z[mine, :] = meta[...]
    rz_old[mine, :] = rows_old[:, pl.ds(half, HALF)]
    rz_new[mine, :] = rows_new[:, pl.ds(pl.multiple_of(zh * 896 + core * 384, 128), WIN)]
    pl.semaphore_wait(barrier, 26)

    def z_copy(o, kind):
        offset = ZOFF[o]
        there = lax.rem(z + offset, 16) // 4
        if kind == 0:
            src, land = meta, meta_z
        elif kind == 1:
            window = pl.ds(pl.multiple_of(there * 896 + core * 384, 128), WIN)
            src, land = rows_new.at[:, window], rz_new
        else:
            src, land = rows_old.at[:, pl.ds(half, HALF)], rz_old
        return remote(src, land.at[mine, :], zs.at[kind, o], zr.at[kind, o], z_dev(offset))

    def z_from(o, kind, buf):
        src = lax.rem(zl + 16 - ZOFF[o], 4)
        ref = buf.at[pl.ds(pl.multiple_of(src * ROWS, ROWS), ROWS), :]
        return remote(ref, ref, zs.at[kind, o], zr.at[kind, o], z_dev(ZOFF[o]))

    for kind in range(3):
        for o in range(3):
            z_copy(o, kind).start()
    for o in range(3):
        z_from(o, 0, meta_z).wait_recv()

    lane = iota((4 * ROWS, 128), 1)
    p_row, p_col = iota((4 * ROWS, 4 * ROWS), 0), iota((4 * ROWS, 4 * ROWS), 1)
    before = jnp.where((p_col < p_row) & (p_col >> 5 == p_row >> 5), 1.0, 0.0).astype(BF)
    qs = iota((16 * SLOTS, 128), 0)
    pick = jnp.where(by24(qs) * 4 + zl == iota((16 * SLOTS, 128), 1), 1.0, 0.0).astype(BF)
    in_q = qs - by24(qs) * 24
    slot_q = (in_q - by6(in_q) * 6).astype(F32)
    same_q = by6(in_q) == iota((16 * SLOTS, 128), 1) >> 5
    ql = iota((128, 16 * SLOTS), 1)
    in_l = ql - by24(ql) * 24
    slot_l = (in_l - by6(in_l) * 6).astype(F32)
    same_l = by6(in_l) == iota((128, 16 * SLOTS), 0) >> 5
    for b in range(2):
        named = jnp.zeros((4 * ROWS, 128), F32)
        gate = jnp.zeros((4 * ROWS, 128), F32)
        for k in range(TOPK):
            hit = meta_z[:, 8 * b + k : 8 * b + k + 1].astype(jnp.int32) == lane
            named = named + jnp.where(hit, 1.0, 0.0)
            gate = gate + jnp.where(hit, meta_z[:, 16 + 8 * b + k : 17 + 8 * b + k], 0.0)
        rank = dot(before, named.astype(BF))
        code = jnp.where(named > 0.5, rank, -1.0).astype(BF)
        disp[b] = jnp.where((dot_nt(pick, code) == slot_q) & same_q, 1.0, 0.0).astype(BF)
        chosen = (dot_nt(code, pick) == slot_l) & same_l
        high = gate.astype(BF)
        low = (gate - high.astype(F32)).astype(BF)
        comb[b, 0] = jnp.where(chosen, dot_nt(high, pick), 0.0).astype(BF)
        comb[b, 1] = jnp.where(chosen, dot_nt(low, pick), 0.0).astype(BF)

    def message_to(b, buf, land, dx, dy):
        d = peer(dx, dy)
        i = 4 * dx + dy
        return remote(buf.at[d], land.at[me], xs.at[b, i], xr.at[b, i], xy_dev(d))

    def message_from(b, land, dx, dy):
        d = peer(4 - dx, 4 - dy)
        i = 4 * dx + dy
        return d, remote(land.at[d], land.at[d], xs.at[b, i], xr.at[b, i], xy_dev(d))

    def put(buf, at, value, width):
        v = value.reshape(4, SLOTS, 2 * width)
        buf[at, 0:SLOTS, :] = v[:, :, :width].astype(BF)
        buf[at, SLOTS : 2 * SLOTS, :] = v[:, :, width:].astype(BF)

    def take(buf, g, h, width):
        v = buf[pl.ds(4 * g, 4), h * SLOTS : (h + 1) * SLOTS, :]
        return v.astype(F32).reshape(CH, width).astype(BF)

    def dispatch(b, rz, buf, land, width):
        for s in ORDER:
            g = lax.rem(x + s, 4)
            table = disp[b, pl.ds(pl.multiple_of(g * CH, 16), CH), :]
            put(buf, pl.ds(4 * g, 4), dot(table, rz[...]), width)
            for dy in (2, 1, 3, 0):
                if (s, dy) == (0, 0):
                    land[me] = buf[me]
                else:
                    message_to(b, buf, land, s, dy).start()

    for o in range(3):
        z_from(o, 1, rz_new).wait_recv()
    dispatch(1, rz_new, send_new, recv_new, WIN // 2)
    for o in range(3):
        z_from(o, 2, rz_old).wait_recv()
    dispatch(0, rz_old, send_old, recv_old, BLK)

    def sx_copy(s):
        return remote(sx_send.at[s], sx_recv.at[s], sxs.at[s], sxr.at[s], sibling)

    def rs_copy(s, k):
        return remote(
            rs_send.at[s, lax.rem(zh + k, 4)], rs_recv.at[s, k - 1],
            rss.at[s, k - 1], rsr.at[s, k - 1], zh_dev(k),
        )

    def act_part(s):
        g = lax.rem(x + 4 - s, 4)
        for dy in (2, 1, 3, 0):
            if (s, dy) != (0, 0):
                message_from(1, recv_new, s, dy)[1].wait_recv()
        rows = [take(recv_new, g, h, WIN // 2) for h in range(2)]

        def part(c):
            return sum(dot(rows[h], w_new[c, h * (WIN // 2) : (h + 1) * (WIN // 2), :]) for h in range(2))

        sx_send[s] = part(1 - core).astype(BF)
        sx_copy(s).start()
        pn_own[s] = part(core)

    def act_send(s):
        sx_copy(s).wait_recv()
        for k in range(4):
            cols = slice(256 * k, 256 * (k + 1))
            rs_send[s, k] = (pn_own[s, :, cols] + sx_recv[s, :, cols].astype(F32)).astype(BF)
        for k in (2, 1, 3):
            rs_copy(s, k).start()

    def so_copy(b, s):
        return remote(so_send.at[b, s], so_recv.at[b, s], sos.at[b, s], sor.at[b, s], sibling)

    def down(b, s, act):
        gate = act[:, :SLAB]
        hidden = (gate / (1.0 + jnp.exp(-gate)) * act[:, SLAB:]).astype(BF)
        so_send[b, s] = dot(hidden, w_out[:, pl.ds(other, HALF)]).astype(BF)
        so_copy(b, s).start()
        po[b, s] = dot(hidden, w_out[:, pl.ds(half, HALF)])

    def back_to(b, dx, dy):
        d = peer(4 - dx, 4 - dy)
        i = 4 * dx + dy
        return remote(ret_send.at[b, d], ret_recv.at[b, me], rts.at[b, i], rtr.at[b, i], xy_dev(d))

    def back_from(b, dx, dy):
        d = peer(dx, dy)
        i = 4 * dx + dy
        return remote(ret_send.at[b, d], ret_recv.at[b, d], rts.at[b, i], rtr.at[b, i], xy_dev(d))

    def back(b, s):
        g = lax.rem(x + 4 - s, 4)
        so_copy(b, s).wait_recv()
        put(ret_send.at[b], pl.ds(4 * g, 4), po[b, s] + so_recv[b, s].astype(F32), BLK)
        for dy in (2, 1, 3, 0):
            if (s, dy) == (0, 0):
                ret_recv[b, me] = ret_send[b, me]
            else:
                back_to(b, s, dy).start()

    for n in range(5):
        if n < 4:
            act_part(ORDER[n])
        if n >= 1:
            act_send(ORDER[n - 1])

    def fwd_copy(s, dy):
        d = peer(4 - s, 4 - dy)
        i = 4 * s + dy
        return remote(recv_old.at[d], sib_old.at[d], fs.at[i], fr.at[i], sibling)

    def forward(s):
        for dy in (2, 1, 3, 0):
            if (s, dy) != (0, 0):
                message_from(0, recv_old, s, dy)[1].wait_recv()
            fwd_copy(s, dy).start()

    def act_old(s):
        g = lax.rem(x + 4 - s, 4)
        act = jnp.zeros((CH, 2 * SLAB), F32)
        for h in range(2):
            at = pl.ds(pl.multiple_of(half + h * BLK, 128), BLK)
            act += dot(take(recv_old, g, h, BLK), w_old[at, :])
        for dy in range(4):
            fwd_copy(s, dy).wait_recv()
        for h in range(2):
            at = pl.ds(pl.multiple_of(other + h * BLK, 128), BLK)
            act += dot(take(sib_old, g, h, BLK), w_old[at, :])
        down(0, s, act)

    for n in range(6):
        if n < 4:
            forward(ORDER[n])
        if 1 <= n < 5:
            act_old(ORDER[n - 1])
        if n >= 2:
            back(0, ORDER[n - 2])

    def act_new(s):
        act = rs_send[s, zh].astype(F32)
        for k in range(1, 4):
            rs_copy(s, k).wait_recv()
            act += rs_recv[s, k - 1].astype(F32)
        down(1, s, act)

    for n in range(5):
        if n < 4:
            act_new(ORDER[n])
        if n >= 1:
            back(1, ORDER[n - 1])

    def z1_copy(b, o):
        at = pl.ds(pl.multiple_of(lax.rem(zl + ZOFF[o], 4) * ROWS, ROWS), ROWS)
        return remote(z1_send.at[b, at, :], z1_recv.at[b, o], z1s.at[b, o], z1r.at[b, o], z_dev(ZOFF[o]))

    def combine(b):
        for i in range(1, 16):
            back_from(b, i // 4, i % 4).wait_recv()
        for h in range(2):
            rows = ret_recv[b, :, h * SLOTS : (h + 1) * SLOTS, :]
            rows = rows.astype(F32).reshape(16 * SLOTS, BLK).astype(BF)
            total = dot(comb[b, 0], rows) + dot(comb[b, 1], rows)
            cols = slice(h * BLK, (h + 1) * BLK)
            z1_own[b, :, cols] = total
            z1_send[b, :, cols] = total.astype(BF)
        for o in range(3):
            z1_copy(b, o).start()

    def z2_copy(b, t):
        k, c = t // 2, t % 2
        return remote(
            z2_send.at[b, :, k * 896 + c * 384 : k * 896 + c * 384 + WIN], z2_recv.at[b, zh],
            z2s.at[b, t], z2r.at[b, zh], {"rep": (2 * core + k) * 2 + c, "ep": ep},
        )

    def is_self(t):
        return rep == (2 * core + t // 2) * 2 + t % 2

    def spread(b):
        total = z1_own[b, mine, :]
        for o in range(3):
            z1_copy(b, o).wait_recv()
            total += z1_recv[b, o].astype(F32)
        z2_send[b] = total.astype(BF)
        for t in range(4):
            k, c = t // 2, t % 2

            @pl.when(jnp.logical_not(is_self(t)))
            def _():
                z2_copy(b, t).start()

            @pl.when(is_self(t))
            def _():
                z2_recv[b, zh] = z2_send[b, :, k * 896 + c * 384 : k * 896 + c * 384 + WIN]

    def finish(b, out):
        for s in range(4):

            @pl.when(jnp.logical_not((zh == s) & (core == zh // 2)))
            def _():
                ref = z2_recv.at[b, s]
                remote(ref, ref, z2s.at[b, 0], z2r.at[b, s], sibling).wait_recv()

        total = sum(z2_recv[b, s].astype(F32) for s in range(4))
        out[...] = jnp.where(core == 0, total[:, :SLICE], total[:, WIN - SLICE :]).astype(BF)

    combine(0)
    spread(0)
    combine(1)
    finish(0, out_old)
    spread(1)
    finish(1, out_new)

    for o in range(3):
        for kind in range(3):
            z_copy(o, kind).wait_send()
        for b in range(2):
            z1_copy(b, o).wait_send()
    for s in range(4):
        sx_copy(s).wait_send()
        for k in range(1, 4):
            rs_copy(s, k).wait_send()
        for dy in range(4):
            fwd_copy(s, dy).wait_send()
        for b in range(2):
            so_copy(b, s).wait_send()
            for dy in range(4):
                if (s, dy) != (0, 0):
                    message_to(b, (send_old, send_new)[b], (recv_old, recv_new)[b], s, dy).wait_send()
                    back_to(b, s, dy).wait_send()
    for b in range(2):
        for t in range(4):

            @pl.when(jnp.logical_not(is_self(t)))
            def _():
                z2_copy(b, t).wait_send()


def body(rows_old, rows_new, routes_old, routes_new, gates_old, gates_new, w_in_old, w_in_new, w_out):
    core = lax.rem(lax.axis_index("rep"), 2)
    meta = jnp.concatenate(
        [routes_old.astype(F32), routes_new.astype(F32), gates_old, gates_new], axis=1
    )
    meta = jnp.pad(meta, ((0, 0), (0, 96)))
    w_old = w_in_old[0].reshape(D, 2 * SLAB)
    w_new = w_in_new[0].reshape(SLICE, 2, 4, 2, SLAB).transpose(3, 0, 2, 1, 4).reshape(2, SLICE, 1024)
    pad = WIN - SLICE
    w_new = jnp.where(
        core == 0, jnp.pad(w_new, ((0, 0), (0, pad), (0, 0))), jnp.pad(w_new, ((0, 0), (pad, 0), (0, 0)))
    )
    vmem = pl.BlockSpec(memory_space=pltpu.VMEM)
    dma = pltpu.SemaphoreType.DMA
    out = jax.ShapeDtypeStruct((ROWS, SLICE), BF)
    return pl.pallas_call(
        kernel,
        out_shape=(out, out),
        in_specs=[vmem] * 6,
        out_specs=(vmem, vmem),
        scratch_shapes=[
            pltpu.VMEM((4 * ROWS, 128), F32),
            pltpu.VMEM((4 * ROWS, HALF), BF),
            pltpu.VMEM((4 * ROWS, WIN), BF),
            pltpu.VMEM((2, 16 * SLOTS, 128), BF),
            pltpu.VMEM((2, 2, 128, 16 * SLOTS), BF),
            pltpu.VMEM((16, 2 * SLOTS, WIN // 2), BF),
            pltpu.VMEM((16, 2 * SLOTS, WIN // 2), BF),
            pltpu.VMEM((16, 2 * SLOTS, BLK), BF),
            pltpu.VMEM((16, 2 * SLOTS, BLK), BF),
            pltpu.VMEM((16, 2 * SLOTS, BLK), BF),
            pltpu.VMEM((4, CH, 1024), F32),
            pltpu.VMEM((4, CH, 1024), BF),
            pltpu.VMEM((4, CH, 1024), BF),
            pltpu.VMEM((4, 4, CH, 256), BF),
            pltpu.VMEM((4, 3, CH, 256), BF),
            pltpu.VMEM((2, 4, CH, HALF), F32),
            pltpu.VMEM((2, 4, CH, HALF), BF),
            pltpu.VMEM((2, 4, CH, HALF), BF),
            pltpu.VMEM((2, 16, 2 * SLOTS, BLK), BF),
            pltpu.VMEM((2, 16, 2 * SLOTS, BLK), BF),
            pltpu.VMEM((2, 4 * ROWS, HALF), F32),
            pltpu.VMEM((2, 4 * ROWS, HALF), BF),
            pltpu.VMEM((2, 3, ROWS, HALF), BF),
            pltpu.VMEM((2, ROWS, HALF), BF),
            pltpu.VMEM((2, 4, ROWS, WIN), BF),
            dma((3, 3)), dma((3, 3)),
            dma((2, 16)), dma((2, 16)),
            dma((16,)), dma((16,)),
            dma((4,)), dma((4,)),
            dma((4, 3)), dma((4, 3)),
            dma((2, 4)), dma((2, 4)),
            dma((2, 16)), dma((2, 16)),
            dma((2, 3)), dma((2, 3)),
            dma((2, 4)), dma((2, 4)),
        ],
        compiler_params=pltpu.CompilerParams(
            collective_id=0, has_side_effects=True, vmem_limit_bytes=60 * 1024 * 1024
        ),
    )(meta, rows_old, rows_new, w_old, w_new, w_out[0])


def solution(mesh):
    return jax.shard_map(
        body,
        mesh=mesh,
        in_specs=(
            P("ep", None),
            P("ep", None),
            P("ep", None),
            P("ep", None),
            P("ep", None),
            P("ep", None),
            P("ep", None, None, "rep"),
            P("ep", "rep", None, None),
            P("ep", "rep", None),
        ),
        out_specs=(P("ep", "rep"), P("ep", "rep")),
        check_vma=False,
    )
```

time: 577 us -> 140 us (0.24)
  the two profiles are of different devices: /device:TPU:7 before, /device:TPU:9 now
where the time goes in v1:
time: 140 us; the launch traced here: 139 us
  Pallas kernels  118 us (84%)
  local copies, waits for them, and re-layouts  16 us (11%)
  other arithmetic  5.07 us (4%)
    pallas_call x1, Pallas kernels, body(): pl.pallas_call(kernel, out_shape=(out, out), in_specs=[vmem] * 6, out_spe...  118 us
    another operation x2, local copies, waits for them, and re-layouts, body(): w_in_new[0].reshape(SLICE, 2, 4, 2, SLAB).transpose(3, 0, 2, 1, 4)  9.2 us
    select_n x1, other arithmetic, body(): jnp.where(core == 0, jnp.pad(w_new, ((0, 0), (0, pad), (0, 0))), jnp.pad(...  4.38 us
    unnamed x15, local copies, waits for them, and re-layouts  4.37 us

profile of v1, /device:TPU:9, one launch (start us, length us, event | category | flops | bytes accessed | tf_op | source)
XLA Modules:
  0.0 139.5 jit_solution(7441103758445037071)
XLA Ops:
  0.6 6.3 %reshape_squeeze.7 = bf16[448,2,4,2,128]{4,3,2,1,0:T(2,128)(2,1)} reshape(bf16[1,448,2,1024]{3,2,1,0:T(2,128)(2,1)} %param.16) | data formatting | bytes 3670016 | tf_op jit(solution)/shard_map/reshape;squeeze | solution.py:397
  6.9 2.9 %copy.25 = bf16[448,2,4,2,128]{4,1,2,0,3:T(2,128)(2,1)S(1)} copy(bf16[448,2,4,2,128]{4,3,2,1,0:T(2,128)(2,1)} %reshape_squeeze.7) | data formatting | bytes 3670016 | tf_op jit(solution)/shard_map/reshape;squeeze | solution.py:397
  9.8 2.3 %reshape.7 = bf16[2,448,1024]{2,1,0:T(8,128)(2,1)} reshape(bf16[2,448,4,2,128]{4,3,2,1,0:T(2,128)(2,1)S(1)} %bitcast.9) | data formatting | bytes 3670016 | tf_op jit(solution)/shard_map/reshape | solution.py:397
  12.1 0.0 copy-start
  12.1 4.4 %pad_select_fusion.w_new = bf16[2,512,1024]{2,1,0:T(8,128)(2,1)} fusion(bf16[2,448,1024]{2,1,0:T(8,128)(2,1)} %reshape.7, pred[]{:T(512)S(6)} %eq.3), kind=kLoop, calls=%fused_computation | loop fusion | flops 1048576 | bytes 3932161 | tf_op jit(solution)/shard_map/jit(_where)/select_n | solution.py:399
  16.5 0.0 copy-done
  16.5 0.0 copy-start.3
  16.5 0.0 copy-start.4
  16.5 0.0 copy-start.1
  16.5 0.0 copy-start.2
  16.5 1.5 %copy.24 = bf16[448,8,2,128]{3,1,2,0:T(8,128)(2,1)} copy(bf16[448,8,2,128]{3,2,1,0:T(2,128)(2,1)S(1)} %bitcast.11) | data formatting | bytes 3670016
  18.0 0.0 copy-done.3
  18.0 0.1 copy.16
  18.0 0.0 copy-done.4
  18.0 0.1 copy.17
  18.1 0.0 copy-done.1
  18.1 0.1 copy.18
  18.2 0.0 copy-done.2
  18.2 0.1 copy.19
  18.3 0.7 select_maximum_fusion.meta
  19.0 117.7 %shard_map.104 = (bf16[32,448]{1,0:T(8,128)(2,1)}, bf16[32,448]{1,0:T(8,128)(2,1)}) custom-call(f32[32,128]{1,0:T(8,128)} %select_maximum_fusion.meta, bf16[32,3584]{1,0:T(8,128)(2,1)} %rows_old.1, bf16[32,3584]{1,0:T(8,128)(2,1)} %rows_new.1, bf16[3584,256]{1,0:T(8,128)(2,1)} %bitcast.10, bf16[2,512,1024]{2,1,0:T(8,128)(2,1)} %pad_select_fusion.w_new, ...), custom_call_target="tpu_custom_call" | custom-call | tf_op jit(solution)/shard_map/pallas_call | solution.py:405
  136.7 1.4 copy.28
  138.1 1.4 copy.29
  (2 shorter events, 0.0 us)
Async XLA Ops:
  12.1 4.4 %copy-start = (bf16[1,3584,2,128]{3,2,1,0:T(2,128)(2,1)S(1)}, bf16[1,3584,2,128]{3,2,1,0:T(2,128)(2,1)}, u32[]{:S(2)}) copy-start(bf16[1,3584,2,128]{3,2,1,0:T(2,128)(2,1)} %param.15) | copy-start | bytes 5505028
  16.5 1.5 %copy-start.3 = (s32[32,8]{0,1:T(8,128)S(1)}, s32[32,8]{0,1:T(8,128)}, u32[]{:S(2)}) copy-start(s32[32,8]{0,1:T(8,128)} %param.11) | copy-start | bytes 3076
  16.5 1.6 %copy-start.4 = (s32[32,8]{0,1:T(8,128)S(1)}, s32[32,8]{0,1:T(8,128)}, u32[]{:S(2)}) copy-start(s32[32,8]{0,1:T(8,128)} %param.12) | copy-start | bytes 3076
  16.5 1.6 %copy-start.1 = (f32[32,8]{0,1:T(8,128)S(1)}, f32[32,8]{0,1:T(8,128)}, u32[]{:S(2)}) copy-start(f32[32,8]{0,1:T(8,128)} %param.13) | copy-start | bytes 3076
  16.5 1.7 %copy-start.2 = (f32[32,8]{0,1:T(8,128)S(1)}, f32[32,8]{0,1:T(8,128)}, u32[]{:S(2)}) copy-start(f32[32,8]{0,1:T(8,128)} %param.14) | copy-start | bytes 3076

commit v2 on v1

--- a/solution.py
+++ b/solution.py
@@ -47,14 +47,14 @@
 
 
 def kernel(
-    meta, rows_old, rows_new, w_old, w_new, w_out,
+    ro_t, rn_t, go_t, gn_t, rows_old, rows_new, w_old_hbm, w_new_hbm, w_out_hbm,
     out_old, out_new,
-    meta_z, rz_old, rz_new, disp, comb,
+    w_raw, w_wide, w_old, w_new, w_out, square, meta_z, rz_old, rz_new, disp, comb,
     send_new, recv_new, send_old, recv_old, sib_old,
     pn_own, sx_send, sx_recv, rs_send, rs_recv,
     po, so_send, so_recv, ret_send, ret_recv,
     z1_own, z1_send, z1_recv, z2_send, z2_recv,
-    zs, zr, xs, xr, fs, fr, sxs, sxr, rss, rsr, sos, sor, rts, rtr, z1s, z1r, z2s, z2r,
+    ws, zs, zr, xs, xr, fs, fr, sxs, sxr, rss, rsr, sos, sor, rts, rtr, z1s, z1r, z2s, z2r,
 ):
     ep = lax.axis_index("ep")
     rep = lax.axis_index("rep")
@@ -82,6 +82,15 @@
         return pltpu.make_async_remote_copy(
             src_ref=src, dst_ref=dst, send_sem=ss, recv_sem=rs, device_id=dev, device_id_type=MESH
         )
+
+    loads = [
+        pltpu.make_async_copy(src, dst, ws.at[i])
+        for i, (src, dst) in enumerate(
+            ((w_new_hbm, w_raw.at[0]), (w_old_hbm, w_raw.at[1]), (w_out_hbm, w_out))
+        )
+    ]
+    for load in loads:
+        load.start()
 
     barrier = pltpu.get_barrier_semaphore()
     for i in range(1, 16):
@@ -95,7 +104,10 @@
     half = pl.multiple_of(core * HALF, 128)
     other = pl.multiple_of((1 - core) * HALF, 128)
     mine = pl.ds(pl.multiple_of(zl * ROWS, ROWS), ROWS)
-    meta_z[mine, :] = meta[...]
+    square[...] = jnp.zeros((128, 128), F32)
+    for i, table in enumerate((ro_t, rn_t, go_t, gn_t)):
+        square[8 * i : 8 * i + 8, 0:ROWS] = table[...].astype(F32)
+    meta_z[mine, :] = square[...].T[:ROWS, :]
     rz_old[mine, :] = rows_old[:, pl.ds(half, HALF)]
     rz_new[mine, :] = rows_new[:, pl.ds(pl.multiple_of(zh * 896 + core * 384, 128), WIN)]
     pl.semaphore_wait(barrier, 26)
@@ -104,7 +116,7 @@
         offset = ZOFF[o]
         there = lax.rem(z + offset, 16) // 4
         if kind == 0:
-            src, land = meta, meta_z
+            src, land = meta_z.at[mine, :], meta_z
         elif kind == 1:
             window = pl.ds(pl.multiple_of(there * 896 + core * 384, 128), WIN)
             src, land = rows_new.at[:, window], rz_new
@@ -188,6 +200,16 @@
         z_from(o, 2, rz_old).wait_recv()
     dispatch(0, rz_old, send_old, recv_old, BLK)
 
+    loads[0].wait()
+    w_wide[...] = w_raw[0].astype(F32)
+    pad = WIN - SLICE
+    w_new[:, pl.ds(pl.multiple_of((1 - core) * SLICE, 64), pad), :] = jnp.zeros((2, pad, 1024), BF)
+    top = pl.ds(pl.multiple_of(core * pad, 64), SLICE)
+    for h in range(8):
+        for g in range(2):
+            col = (h // 2) * 256 + g * SLAB
+            w_new[h % 2, top, col : col + SLAB] = w_wide[pl.ds(2 * h + g, SLICE, stride=16), :].astype(BF)
+
     def sx_copy(s):
         return remote(sx_send.at[s], sx_recv.at[s], sxs.at[s], sxr.at[s], sibling)
 
@@ -278,6 +300,12 @@
             at = pl.ds(pl.multiple_of(other + h * BLK, 128), BLK)
             act += dot(take(sib_old, g, h, BLK), w_old[at, :])
         down(0, s, act)
+
+    loads[1].wait()
+    w_wide[...] = w_raw[1].astype(F32)
+    for g in range(2):
+        w_old[:, g * SLAB : (g + 1) * SLAB] = w_wide[pl.ds(g, D, stride=2), :].astype(BF)
+    loads[2].wait()
 
     for n in range(6):
         if n < 4:
@@ -388,26 +416,23 @@
 
 
 def body(rows_old, rows_new, routes_old, routes_new, gates_old, gates_new, w_in_old, w_in_new, w_out):
-    core = lax.rem(lax.axis_index("rep"), 2)
-    meta = jnp.concatenate(
-        [routes_old.astype(F32), routes_new.astype(F32), gates_old, gates_new], axis=1
-    )
-    meta = jnp.pad(meta, ((0, 0), (0, 96)))
-    w_old = w_in_old[0].reshape(D, 2 * SLAB)
-    w_new = w_in_new[0].reshape(SLICE, 2, 4, 2, SLAB).transpose(3, 0, 2, 1, 4).reshape(2, SLICE, 1024)
-    pad = WIN - SLICE
-    w_new = jnp.where(
-        core == 0, jnp.pad(w_new, ((0, 0), (0, pad), (0, 0))), jnp.pad(w_new, ((0, 0), (pad, 0), (0, 0)))
-    )
+    w_old = w_in_old[0].reshape(2 * D, SLAB)
+    w_new = w_in_new[0].reshape(SLICE, 2, 8, SLAB).transpose(0, 2, 1, 3).reshape(SLICE * 16, SLAB)
     vmem = pl.BlockSpec(memory_space=pltpu.VMEM)
     dma = pltpu.SemaphoreType.DMA
     out = jax.ShapeDtypeStruct((ROWS, SLICE), BF)
     return pl.pallas_call(
         kernel,
         out_shape=(out, out),
-        in_specs=[vmem] * 6,
+        in_specs=[vmem] * 6 + [pl.BlockSpec(memory_space=pl.ANY)] * 3,
         out_specs=(vmem, vmem),
         scratch_shapes=[
+            pltpu.VMEM((2, 2 * D, SLAB), BF),
+            pltpu.VMEM((2 * D, SLAB), F32),
+            pltpu.VMEM((D, 2 * SLAB), BF),
+            pltpu.VMEM((2, WIN, 1024), BF),
+            pltpu.VMEM((SLAB, D), BF),
+            pltpu.VMEM((128, 128), F32),
             pltpu.VMEM((4 * ROWS, 128), F32),
             pltpu.VMEM((4 * ROWS, HALF), BF),
             pltpu.VMEM((4 * ROWS, WIN), BF),
@@ -433,6 +458,7 @@
             pltpu.VMEM((2, 3, ROWS, HALF), BF),
             pltpu.VMEM((2, ROWS, HALF), BF),
             pltpu.VMEM((2, 4, ROWS, WIN), BF),
+            dma((3,)),
             dma((3, 3)), dma((3, 3)),
             dma((2, 16)), dma((2, 16)),
             dma((16,)), dma((16,)),
@@ -446,7 +472,7 @@
         compiler_params=pltpu.CompilerParams(
             collective_id=0, has_side_effects=True, vmem_limit_bytes=60 * 1024 * 1024
         ),
-    )(meta, rows_old, rows_new, w_old, w_new, w_out[0])
+    )(routes_old.T, routes_new.T, gates_old.T, gates_new.T, rows_old, rows_new, w_old, w_new, w_out[0])
 
 
 def solution(mesh):

time: 140 us -> 122 us (0.87)
  local copies, waits for them, and re-layouts: 16 us -> 2.75 us
  other arithmetic: 5.07 us -> 0 us
    another operation x2 -> x0, local copies, waits for them, and re-layouts: 9.2 us -> none  [body(): w_in_new[0].reshape(SLICE, 2, 4, 2, SLAB).transpose(3, 0, 2, 1, 4)]
    select_n x1 -> x0, other arithmetic: 4.38 us -> none  [body(): jnp.where(core == 0, jnp.pad(w_new, ((0, 0), (0, pad), (0, 0))), jnp.pad(...]
    reshape x1 -> x0, local copies, waits for them, and re-layouts: 2.26 us -> none  [body(): w_in_new[0].reshape(SLICE, 2, 4, 2, SLAB).transpose(3, 0, 2, 1, 4)]
    unnamed x15 -> x2, local copies, waits for them, and re-layouts: 4.37 us -> 2.75 us
where the time goes in v2:
time: 122 us
  Pallas kernels  119 us (98%)
  local copies, waits for them, and re-layouts  2.75 us (2%)
    pallas_call x1, Pallas kernels, body(): pl.pallas_call(kernel, out_shape=(out, out), in_specs=[vmem] * 6 + [pl.Bl...  119 us
    unnamed x2, local copies, waits for them, and re-layouts  2.75 us

profile of v2, /device:TPU:9, one launch (start us, length us, event | category | flops | bytes accessed | tf_op | source)
XLA Modules:
  0.0 121.9 jit_solution(2567456404382440156)
XLA Ops:
  0.6 118.5 %shard_map.104 = (bf16[32,448]{1,0:T(8,128)(2,1)}, bf16[32,448]{1,0:T(8,128)(2,1)}) custom-call(s32[8,32]{1,0:T(8,128)} %bitcast.14, s32[8,32]{1,0:T(8,128)} %bitcast.15, f32[8,32]{1,0:T(8,128)} %bitcast.16, f32[8,32]{1,0:T(8,128)} %bitcast.17, bf16[32,3584]{1,0:T(8,128)(2,1)} %rows_old.1, bf16[32,3584]{1,0:T(8,128)(2,1)} %rows_new.1, ...), custom_call_target="tpu_custom_call" | custom-call | tf_op jit(solution)/shard_map/pallas_call | solution.py:424
  119.2 1.4 %copy.14 = bf16[32,448]{1,0:T(8,128)(2,1)} copy(bf16[32,448]{1,0:T(8,128)(2,1)} %get-tuple-element.4) | data formatting | bytes 57344
  120.5 1.4 %copy.15 = bf16[32,448]{1,0:T(8,128)(2,1)} copy(bf16[32,448]{1,0:T(8,128)(2,1)} %get-tuple-element.5) | data formatting | bytes 57344

commit v3 on v2

--- a/solution.py
+++ b/solution.py
@@ -22,7 +22,10 @@
 CAP = 6
 SLOTS = 4 * CAP
 CH = 4 * SLOTS
-ORDER = (2, 1, 3, 0)
+FAR = (2, 1, 3, 0)
+PLACE = tuple((dx, (total - dx) % 4) for total in FAR for dx in FAR)
+PART_A, PART_B = 512, 384
+PARTS = ((0, PART_A), (2 * PART_A, PART_B))
 ZOFF = (1, 15, 2)
 
 
@@ -44,6 +47,10 @@
 
 def by6(q):
     return (q * 10923) >> 16
+
+
+def far(m):
+    return jnp.where(m == 0, 2, jnp.where(m == 3, 0, 2 * m - 1))
 
 
 def kernel(
@@ -51,10 +58,10 @@
     out_old, out_new,
     w_raw, w_wide, w_old, w_new, w_out, square, meta_z, rz_old, rz_new, disp, comb,
     send_new, recv_new, send_old, recv_old, sib_old,
-    pn_own, sx_send, sx_recv, rs_send, rs_recv,
-    po, so_send, so_recv, ret_send, ret_recv,
+    pn, sx_send, sx_recv, rf_send, rf_recv, rn_send, rn_recv,
+    po, so_send, so_recv, ra_send, ra_recv, rb_send, rb_recv,
     z1_own, z1_send, z1_recv, z2_send, z2_recv,
-    ws, zs, zr, xs, xr, fs, fr, sxs, sxr, rss, rsr, sos, sor, rts, rtr, z1s, z1r, z2s, z2r,
+    ws, zs, zr, xs, xr, fs, fr, sxs, sxr, rfs, rfr, rns, rnr, sos, sor, rts, rtr, z1s, z1r, z2s, z2r,
 ):
     ep = lax.axis_index("ep")
     rep = lax.axis_index("rep")
@@ -67,11 +74,13 @@
         t = lax.rem(z + offset, 16)
         return {"rep": (t // 4) * 2 + core, "ep": me * 4 + lax.rem(t, 4)}
 
-    def peer(dx, dy):
-        return lax.rem(x + dx, 4) * 4 + lax.rem(y + dy, 4)
-
-    def xy_dev(d):
-        return {"rep": rep, "ep": d * 4 + zl}
+    def to_dev(r):
+        dx, dy = PLACE[r]
+        return {"rep": rep, "ep": (lax.rem(x + dx, 4) * 4 + lax.rem(y + dy, 4)) * 4 + zl}
+
+    def from_dev(r):
+        dx, dy = PLACE[r]
+        return {"rep": rep, "ep": (lax.rem(x + 4 - dx, 4) * 4 + lax.rem(y + 4 - dy, 4)) * 4 + zl}
 
     def zh_dev(k):
         return {"rep": lax.rem(zh + k, 4) * 2 + core, "ep": ep}
@@ -93,8 +102,8 @@
         load.start()
 
     barrier = pltpu.get_barrier_semaphore()
-    for i in range(1, 16):
-        pl.semaphore_signal(barrier, 1, device_id=xy_dev(peer(i // 4, i % 4)), device_id_type=MESH)
+    for r in range(15):
+        pl.semaphore_signal(barrier, 1, device_id=to_dev(r), device_id_type=MESH)
     for o in (1, 15, 2, 14):
         pl.semaphore_signal(barrier, 1, device_id=z_dev(o), device_id_type=MESH)
     for k in range(1, 8):
@@ -139,7 +148,11 @@
     p_row, p_col = iota((4 * ROWS, 4 * ROWS), 0), iota((4 * ROWS, 4 * ROWS), 1)
     before = jnp.where((p_col < p_row) & (p_col >> 5 == p_row >> 5), 1.0, 0.0).astype(BF)
     qs = iota((16 * SLOTS, 128), 0)
-    pick = jnp.where(by24(qs) * 4 + zl == iota((16 * SLOTS, 128), 1), 1.0, 0.0).astype(BF)
+    rq = by24(qs)
+    dx = far(rq & 3)
+    dy = (far(rq >> 2) - dx) & 3
+    expert = (((x + dx) & 3) * 4 + ((y + dy) & 3)) * 4 + zl
+    pick = jnp.where(expert == iota((16 * SLOTS, 128), 1), 1.0, 0.0).astype(BF)
     in_q = qs - by24(qs) * 24
     slot_q = (in_q - by6(in_q) * 6).astype(F32)
     same_q = by6(in_q) == iota((16 * SLOTS, 128), 1) >> 5
@@ -163,35 +176,26 @@
         comb[b, 0] = jnp.where(chosen, dot_nt(high, pick), 0.0).astype(BF)
         comb[b, 1] = jnp.where(chosen, dot_nt(low, pick), 0.0).astype(BF)
 
-    def message_to(b, buf, land, dx, dy):
-        d = peer(dx, dy)
-        i = 4 * dx + dy
-        return remote(buf.at[d], land.at[me], xs.at[b, i], xr.at[b, i], xy_dev(d))
-
-    def message_from(b, land, dx, dy):
-        d = peer(4 - dx, 4 - dy)
-        i = 4 * dx + dy
-        return d, remote(land.at[d], land.at[d], xs.at[b, i], xr.at[b, i], xy_dev(d))
-
-    def put(buf, at, value, width):
+    def message(b, buf, land, r):
+        return remote(buf.at[r], land.at[r], xs.at[b, r], xr.at[b, r], to_dev(r))
+
+    def put(buf, n, value, width):
         v = value.reshape(4, SLOTS, 2 * width)
-        buf[at, 0:SLOTS, :] = v[:, :, :width].astype(BF)
-        buf[at, SLOTS : 2 * SLOTS, :] = v[:, :, width:].astype(BF)
-
-    def take(buf, g, h, width):
-        v = buf[pl.ds(4 * g, 4), h * SLOTS : (h + 1) * SLOTS, :]
+        buf[4 * n : 4 * n + 4, 0:SLOTS, :] = v[:, :, :width].astype(BF)
+        buf[4 * n : 4 * n + 4, SLOTS : 2 * SLOTS, :] = v[:, :, width:].astype(BF)
+
+    def take(buf, n, h, width):
+        v = buf[4 * n : 4 * n + 4, h * SLOTS : (h + 1) * SLOTS, :]
         return v.astype(F32).reshape(CH, width).astype(BF)
 
     def dispatch(b, rz, buf, land, width):
-        for s in ORDER:
-            g = lax.rem(x + s, 4)
-            table = disp[b, pl.ds(pl.multiple_of(g * CH, 16), CH), :]
-            put(buf, pl.ds(4 * g, 4), dot(table, rz[...]), width)
-            for dy in (2, 1, 3, 0):
-                if (s, dy) == (0, 0):
-                    land[me] = buf[me]
+        for n in range(4):
+            put(buf, n, dot(disp[b, n * CH : (n + 1) * CH, :], rz[...]), width)
+            for r in range(4 * n, 4 * n + 4):
+                if r < 15:
+                    message(b, buf, land, r).start()
                 else:
-                    message_to(b, buf, land, s, dy).start()
+                    land[15] = buf[15]
 
     for o in range(3):
         z_from(o, 1, rz_new).wait_recv()
@@ -207,99 +211,104 @@
     top = pl.ds(pl.multiple_of(core * pad, 64), SLICE)
     for h in range(8):
         for g in range(2):
-            col = (h // 2) * 256 + g * SLAB
-            w_new[h % 2, top, col : col + SLAB] = w_wide[pl.ds(2 * h + g, SLICE, stride=16), :].astype(BF)
-
-    def sx_copy(s):
-        return remote(sx_send.at[s], sx_recv.at[s], sxs.at[s], sxr.at[s], sibling)
-
-    def rs_copy(s, k):
-        return remote(
-            rs_send.at[s, lax.rem(zh + k, 4)], rs_recv.at[s, k - 1],
-            rss.at[s, k - 1], rsr.at[s, k - 1], zh_dev(k),
-        )
-
-    def act_part(s):
-        g = lax.rem(x + 4 - s, 4)
-        for dy in (2, 1, 3, 0):
-            if (s, dy) != (0, 0):
-                message_from(1, recv_new, s, dy)[1].wait_recv()
-        rows = [take(recv_new, g, h, WIN // 2) for h in range(2)]
+            col = pl.multiple_of(lax.rem(h // 2 + 4 - zh, 4) * 256 + g * SLAB, SLAB)
+            w_new[h % 2, top, pl.ds(col, SLAB)] = w_wide[pl.ds(2 * h + g, SLICE, stride=16), :].astype(BF)
+
+    def sx_copy(n):
+        return remote(sx_send.at[n], sx_recv.at[n], sxs.at[n], sxr.at[n], sibling)
+
+    def rf_copy(n, i):
+        return remote(rf_send.at[n, i], rf_recv.at[n, i], rfs.at[n, i], rfr.at[n, i], zh_dev(1 + 2 * i))
+
+    def rn_copy(n, i):
+        return remote(rn_send.at[n, i], rn_recv.at[n, i], rns.at[n, i], rnr.at[n, i], zh_dev(1 + 2 * i))
+
+    def act_part(n):
+        for r in range(4 * n, min(4 * n + 4, 15)):
+            message(1, send_new, recv_new, r).wait_recv()
+        rows = [take(recv_new, n, h, WIN // 2) for h in range(2)]
 
         def part(c):
             return sum(dot(rows[h], w_new[c, h * (WIN // 2) : (h + 1) * (WIN // 2), :]) for h in range(2))
 
-        sx_send[s] = part(1 - core).astype(BF)
-        sx_copy(s).start()
-        pn_own[s] = part(core)
-
-    def act_send(s):
-        sx_copy(s).wait_recv()
-        for k in range(4):
-            cols = slice(256 * k, 256 * (k + 1))
-            rs_send[s, k] = (pn_own[s, :, cols] + sx_recv[s, :, cols].astype(F32)).astype(BF)
-        for k in (2, 1, 3):
-            rs_copy(s, k).start()
-
-    def so_copy(b, s):
-        return remote(so_send.at[b, s], so_recv.at[b, s], sos.at[b, s], sor.at[b, s], sibling)
-
-    def down(b, s, act):
+        sx_send[n] = part(1 - core).astype(BF)
+        sx_copy(n).start()
+        pn[n] = part(core)
+
+    def act_far(n):
+        sx_copy(n).wait_recv()
+        total = pn[n] + sx_recv[n].astype(F32)
+        for i in range(2):
+            rf_send[n, i] = total[i * CH // 2 : (i + 1) * CH // 2, 512:768].astype(BF)
+            rf_copy(n, i).start()
+        pn[n] = total
+
+    def act_near(n):
+        for i in range(2):
+            rf_copy(n, i).wait_recv()
+            cols = slice(256 + 512 * i, 512 + 512 * i)
+            own, more = slice((1 - i) * CH // 2, (2 - i) * CH // 2), slice(i * CH // 2, (i + 1) * CH // 2)
+            rn_send[n, i, own, :] = pn[n, own, cols].astype(BF)
+            rn_send[n, i, more, :] = (pn[n, more, cols] + rf_recv[n, i].astype(F32)).astype(BF)
+            rn_copy(n, i).start()
+
+    def so_copy(b, n):
+        return remote(so_send.at[b, n], so_recv.at[b, n], sos.at[b, n], sor.at[b, n], sibling)
+
+    def down(b, n, act):
         gate = act[:, :SLAB]
         hidden = (gate / (1.0 + jnp.exp(-gate)) * act[:, SLAB:]).astype(BF)
-        so_send[b, s] = dot(hidden, w_out[:, pl.ds(other, HALF)]).astype(BF)
-        so_copy(b, s).start()
-        po[b, s] = dot(hidden, w_out[:, pl.ds(half, HALF)])
-
-    def back_to(b, dx, dy):
-        d = peer(4 - dx, 4 - dy)
-        i = 4 * dx + dy
-        return remote(ret_send.at[b, d], ret_recv.at[b, me], rts.at[b, i], rtr.at[b, i], xy_dev(d))
-
-    def back_from(b, dx, dy):
-        d = peer(dx, dy)
-        i = 4 * dx + dy
-        return remote(ret_send.at[b, d], ret_recv.at[b, d], rts.at[b, i], rtr.at[b, i], xy_dev(d))
-
-    def back(b, s):
-        g = lax.rem(x + 4 - s, 4)
-        so_copy(b, s).wait_recv()
-        put(ret_send.at[b], pl.ds(4 * g, 4), po[b, s] + so_recv[b, s].astype(F32), BLK)
-        for dy in (2, 1, 3, 0):
-            if (s, dy) == (0, 0):
-                ret_recv[b, me] = ret_send[b, me]
+        so_send[b, n] = dot(hidden, w_out[:, pl.ds(other, HALF)]).astype(BF)
+        so_copy(b, n).start()
+        po[b, n] = dot(hidden, w_out[:, pl.ds(half, HALF)])
+
+    def back(b, part, r):
+        src, land = ((ra_send, ra_recv), (rb_send, rb_recv))[part]
+        return remote(src.at[b, r], land.at[b, r], rts.at[b, part, r], rtr.at[b, part, r], from_dev(r))
+
+    def chip_sum(b, n):
+        so_copy(b, n).wait_recv()
+        total = po[b, n] + so_recv[b, n].astype(F32)
+        put(ra_send.at[b], n, total[:, : 2 * PART_A], PART_A)
+        put(rb_send.at[b], n, total[:, 2 * PART_A :], PART_B)
+
+    def send_back(b, part, n):
+        for r in range(4 * n, 4 * n + 4):
+            if r < 15:
+                back(b, part, r).start()
+            elif part == 0:
+                ra_recv[b, 15] = ra_send[b, 15]
             else:
-                back_to(b, s, dy).start()
-
-    for n in range(5):
+                rb_recv[b, 15] = rb_send[b, 15]
+
+    for n in range(6):
         if n < 4:
-            act_part(ORDER[n])
-        if n >= 1:
-            act_send(ORDER[n - 1])
-
-    def fwd_copy(s, dy):
-        d = peer(4 - s, 4 - dy)
-        i = 4 * s + dy
-        return remote(recv_old.at[d], sib_old.at[d], fs.at[i], fr.at[i], sibling)
-
-    def forward(s):
-        for dy in (2, 1, 3, 0):
-            if (s, dy) != (0, 0):
-                message_from(0, recv_old, s, dy)[1].wait_recv()
-            fwd_copy(s, dy).start()
-
-    def act_old(s):
-        g = lax.rem(x + 4 - s, 4)
+            act_part(n)
+        if 1 <= n < 5:
+            act_far(n - 1)
+        if n >= 2:
+            act_near(n - 2)
+
+    def fwd_copy(r):
+        return remote(recv_old.at[r], sib_old.at[r], fs.at[r], fr.at[r], sibling)
+
+    def forward(n):
+        for r in range(4 * n, 4 * n + 4):
+            if r < 15:
+                message(0, send_old, recv_old, r).wait_recv()
+            fwd_copy(r).start()
+
+    def act_old(n):
         act = jnp.zeros((CH, 2 * SLAB), F32)
         for h in range(2):
             at = pl.ds(pl.multiple_of(half + h * BLK, 128), BLK)
-            act += dot(take(recv_old, g, h, BLK), w_old[at, :])
-        for dy in range(4):
-            fwd_copy(s, dy).wait_recv()
+            act += dot(take(recv_old, n, h, BLK), w_old[at, :])
+        for r in range(4 * n, 4 * n + 4):
+            fwd_copy(r).wait_recv()
         for h in range(2):
             at = pl.ds(pl.multiple_of(other + h * BLK, 128), BLK)
-            act += dot(take(sib_old, g, h, BLK), w_old[at, :])
-        down(0, s, act)
+            act += dot(take(sib_old, n, h, BLK), w_old[at, :])
+        down(0, n, act)
 
     loads[1].wait()
     w_wide[...] = w_raw[1].astype(F32)
@@ -309,41 +318,52 @@
 
     for n in range(6):
         if n < 4:
-            forward(ORDER[n])
+            forward(n)
         if 1 <= n < 5:
-            act_old(ORDER[n - 1])
+            act_old(n - 1)
         if n >= 2:
-            back(0, ORDER[n - 2])
-
-    def act_new(s):
-        act = rs_send[s, zh].astype(F32)
-        for k in range(1, 4):
-            rs_copy(s, k).wait_recv()
-            act += rs_recv[s, k - 1].astype(F32)
-        down(1, s, act)
-
-    for n in range(5):
+            chip_sum(0, n - 2)
+            send_back(0, 0, n - 2)
+            send_back(0, 1, n - 2)
+
+    def act_new(n):
+        act = pn[n, :, 0:256]
+        for i in range(2):
+            rn_copy(n, i).wait_recv()
+            act += rn_recv[n, i].astype(F32)
+        down(1, n, act)
+
+    for n in range(6):
         if n < 4:
-            act_new(ORDER[n])
-        if n >= 1:
-            back(1, ORDER[n - 1])
-
-    def z1_copy(b, o):
+            act_new(n)
+        if 1 <= n < 5:
+            chip_sum(1, n - 1)
+            send_back(1, 0, n - 1)
+        if n >= 2:
+            send_back(1, 1, n - 2)
+
+    def z1_copy(b, part, o):
         at = pl.ds(pl.multiple_of(lax.rem(zl + ZOFF[o], 4) * ROWS, ROWS), ROWS)
-        return remote(z1_send.at[b, at, :], z1_recv.at[b, o], z1s.at[b, o], z1r.at[b, o], z_dev(ZOFF[o]))
-
-    def combine(b):
-        for i in range(1, 16):
-            back_from(b, i // 4, i % 4).wait_recv()
+        col, width = PARTS[part]
+        cols = slice(col, col + 2 * width)
+        return remote(
+            z1_send.at[b, at, cols], z1_recv.at[b, o, :, cols],
+            z1s.at[b, part, o], z1r.at[b, part, o], z_dev(ZOFF[o]),
+        )
+
+    def combine(b, part):
+        for r in range(15):
+            back(b, part, r).wait_recv()
+        col, width = PARTS[part]
         for h in range(2):
-            rows = ret_recv[b, :, h * SLOTS : (h + 1) * SLOTS, :]
-            rows = rows.astype(F32).reshape(16 * SLOTS, BLK).astype(BF)
+            rows = (ra_recv, rb_recv)[part][b, :, h * SLOTS : (h + 1) * SLOTS, :]
+            rows = rows.astype(F32).reshape(16 * SLOTS, width).astype(BF)
             total = dot(comb[b, 0], rows) + dot(comb[b, 1], rows)
-            cols = slice(h * BLK, (h + 1) * BLK)
+            cols = slice(col + h * width, col + (h + 1) * width)
             z1_own[b, :, cols] = total
             z1_send[b, :, cols] = total.astype(BF)
         for o in range(3):
-            z1_copy(b, o).start()
+            z1_copy(b, part, o).start()
 
     def z2_copy(b, t):
         k, c = t // 2, t % 2
@@ -355,13 +375,15 @@
     def is_self(t):
         return rep == (2 * core + t // 2) * 2 + t % 2
 
-    def spread(b):
-        total = z1_own[b, mine, :]
+    def spread(b, part):
+        col, width = PARTS[part]
+        cols = slice(col, col + 2 * width)
+        total = z1_own[b, mine, cols]
         for o in range(3):
-            z1_copy(b, o).wait_recv()
-            total += z1_recv[b, o].astype(F32)
-        z2_send[b] = total.astype(BF)
-        for t in range(4):
+            z1_copy(b, part, o).wait_recv()
+            total += z1_recv[b, o, :, cols].astype(F32)
+        z2_send[b, :, cols] = total.astype(BF)
+        for t in (2 * part, 2 * part + 1):
             k, c = t // 2, t % 2
 
             @pl.when(jnp.logical_not(is_self(t)))
@@ -383,30 +405,38 @@
         total = sum(z2_recv[b, s].astype(F32) for s in range(4))
         out[...] = jnp.where(core == 0, total[:, :SLICE], total[:, WIN - SLICE :]).astype(BF)
 
-    combine(0)
-    spread(0)
-    combine(1)
+    combine(0, 0)
+    combine(0, 1)
+    spread(0, 0)
+    spread(0, 1)
     finish(0, out_old)
-    spread(1)
+    combine(1, 0)
+    spread(1, 0)
+    combine(1, 1)
+    spread(1, 1)
     finish(1, out_new)
 
     for o in range(3):
         for kind in range(3):
             z_copy(o, kind).wait_send()
         for b in range(2):
-            z1_copy(b, o).wait_send()
-    for s in range(4):
-        sx_copy(s).wait_send()
-        for k in range(1, 4):
-            rs_copy(s, k).wait_send()
-        for dy in range(4):
-            fwd_copy(s, dy).wait_send()
+            for part in range(2):
+                z1_copy(b, part, o).wait_send()
+    for n in range(4):
+        sx_copy(n).wait_send()
+        for i in range(2):
+            rf_copy(n, i).wait_send()
+            rn_copy(n, i).wait_send()
         for b in range(2):
-            so_copy(b, s).wait_send()
-            for dy in range(4):
-                if (s, dy) != (0, 0):
-                    message_to(b, (send_old, send_new)[b], (recv_old, recv_new)[b], s, dy).wait_send()
-                    back_to(b, s, dy).wait_send()
+            so_copy(b, n).wait_send()
+    for r in range(16):
+        fwd_copy(r).wait_send()
+    for r in range(15):
+        message(0, send_old, recv_old, r).wait_send()
+        message(1, send_new, recv_new, r).wait_send()
+        for b in range(2):
+            for part in range(2):
+                back(b, part, r).wait_send()
     for b in range(2):
         for t in range(4):
 
@@ -446,13 +476,17 @@
             pltpu.VMEM((4, CH, 1024), F32),
             pltpu.VMEM((4, CH, 1024), BF),
             pltpu.VMEM((4, CH, 1024), BF),
-            pltpu.VMEM((4, 4, CH, 256), BF),
-            pltpu.VMEM((4, 3, CH, 256), BF),
+            pltpu.VMEM((4, 2, CH // 2, 256), BF),
+            pltpu.VMEM((4, 2, CH // 2, 256), BF),
+            pltpu.VMEM((4, 2, CH, 256), BF),
+            pltpu.VMEM((4, 2, CH, 256), BF),
             pltpu.VMEM((2, 4, CH, HALF), F32),
             pltpu.VMEM((2, 4, CH, HALF), BF),
             pltpu.VMEM((2, 4, CH, HALF), BF),
-            pltpu.VMEM((2, 16, 2 * SLOTS, BLK), BF),
-            pltpu.VMEM((2, 16, 2 * SLOTS, BLK), BF),
+            pltpu.VMEM((2, 16, 2 * SLOTS, PART_A), BF),
+            pltpu.VMEM((2, 16, 2 * SLOTS, PART_A), BF),
+            pltpu.VMEM((2, 16, 2 * SLOTS, PART_B), BF),
+            pltpu.VMEM((2, 16, 2 * SLOTS, PART_B), BF),
             pltpu.VMEM((2, 4 * ROWS, HALF), F32),
             pltpu.VMEM((2, 4 * ROWS, HALF), BF),
             pltpu.VMEM((2, 3, ROWS, HALF), BF),
@@ -463,10 +497,11 @@
             dma((2, 16)), dma((2, 16)),
             dma((16,)), dma((16,)),
             dma((4,)), dma((4,)),
-            dma((4, 3)), dma((4, 3)),
+            dma((4, 2)), dma((4, 2)),
+            dma((4, 2)), dma((4, 2)),
             dma((2, 4)), dma((2, 4)),
-            dma((2, 16)), dma((2, 16)),
-            dma((2, 3)), dma((2, 3)),
+            dma((2, 2, 16)), dma((2, 2, 16)),
+            dma((2, 2, 3)), dma((2, 2, 3)),
             dma((2, 4)), dma((2, 4)),
         ],
         compiler_params=pltpu.CompilerParams(

time: 122 us -> 136 us (1.11)
  the two profiles are of different devices: /device:TPU:9 before, /device:TPU:171 now
where the time goes in v3:
time: 136 us; the launch traced here: 135 us
  Pallas kernels  132 us (97%)
  local copies, waits for them, and re-layouts  2.75 us (2%)
    pallas_call x1, Pallas kernels, body(): pl.pallas_call(kernel, out_shape=(out, out), in_specs=[vmem] * 6 + [pl.Bl...  132 us
    unnamed x2, local copies, waits for them, and re-layouts  2.75 us

profile of v3, /device:TPU:171, one launch (start us, length us, event | category | flops | bytes accessed | tf_op | source)
XLA Modules:
  0.0 135.5 jit_solution(5303857851273254166)
XLA Ops:
  0.6 132.1 %shard_map.104 = (bf16[32,448]{1,0:T(8,128)(2,1)}, bf16[32,448]{1,0:T(8,128)(2,1)}) custom-call(s32[8,32]{1,0:T(8,128)} %bitcast.14, s32[8,32]{1,0:T(8,128)} %bitcast.15, f32[8,32]{1,0:T(8,128)} %bitcast.16, f32[8,32]{1,0:T(8,128)} %bitcast.17, bf16[32,3584]{1,0:T(8,128)(2,1)} %rows_old.1, bf16[32,3584]{1,0:T(8,128)(2,1)} %rows_new.1, ...), custom_call_target="tpu_custom_call" | custom-call | tf_op jit(solution)/shard_map/pallas_call | solution.py:454
  132.7 1.4 %copy.14 = bf16[32,448]{1,0:T(8,128)(2,1)} copy(bf16[32,448]{1,0:T(8,128)(2,1)} %get-tuple-element.4) | data formatting | bytes 57344
  134.1 1.4 %copy.15 = bf16[32,448]{1,0:T(8,128)(2,1)} copy(bf16[32,448]{1,0:T(8,128)(2,1)} %get-tuple-element.5) | data formatting | bytes 57344

commit v4 on v3

--- a/solution.py
+++ b/solution.py
@@ -23,10 +23,9 @@
 SLOTS = 4 * CAP
 CH = 4 * SLOTS
 FAR = (2, 1, 3, 0)
-PLACE = tuple((dx, (total - dx) % 4) for total in FAR for dx in FAR)
+PLACE = tuple((dx, dy) for dx in FAR for dy in FAR)
 PART_A, PART_B = 512, 384
 PARTS = ((0, PART_A), (2 * PART_A, PART_B))
-ZOFF = (1, 15, 2)
 
 
 def dot(a, b):
@@ -56,12 +55,13 @@
 def kernel(
     ro_t, rn_t, go_t, gn_t, rows_old, rows_new, w_old_hbm, w_new_hbm, w_out_hbm,
     out_old, out_new,
+    tab_i, tab_f, result,
     w_raw, w_wide, w_old, w_new, w_out, square, meta_z, rz_old, rz_new, disp, comb,
     send_new, recv_new, send_old, recv_old, sib_old,
     pn, sx_send, sx_recv, rf_send, rf_recv, rn_send, rn_recv,
     po, so_send, so_recv, ra_send, ra_recv, rb_send, rb_recv,
     z1_own, z1_send, z1_recv, z2_send, z2_recv,
-    ws, zs, zr, xs, xr, fs, fr, sxs, sxr, rfs, rfr, rns, rnr, sos, sor, rts, rtr, z1s, z1r, z2s, z2r,
+    ins, ws, zs, zr, xs, xr, fs, fr, sxs, sxr, rfs, rfr, rns, rnr, sos, sor, rts, rtr, z1s, z1r, z2s, z2r,
 ):
     ep = lax.axis_index("ep")
     rep = lax.axis_index("rep")
@@ -69,6 +69,7 @@
     zl, me = lax.rem(ep, 4), ep // 4
     x, y = me // 4, lax.rem(me, 4)
     z = zh * 4 + zl
+    zoff = (1, 15, 2 + 12 * core)
 
     def z_dev(offset):
         t = lax.rem(z + offset, 16)
@@ -92,14 +93,22 @@
             src_ref=src, dst_ref=dst, send_sem=ss, recv_sem=rs, device_id=dev, device_id_type=MESH
         )
 
-    loads = [
-        pltpu.make_async_copy(src, dst, ws.at[i])
+    half = pl.multiple_of(core * HALF, 128)
+    other = pl.multiple_of((1 - core) * HALF, 128)
+    mine = pl.ds(pl.multiple_of(zl * ROWS, ROWS), ROWS)
+    window = pl.ds(pl.multiple_of(zh * 896 + core * 384, 128), WIN)
+    inputs = [
+        pltpu.make_async_copy(src, dst, ins.at[i])
         for i, (src, dst) in enumerate(
-            ((w_new_hbm, w_raw.at[0]), (w_old_hbm, w_raw.at[1]), (w_out_hbm, w_out))
+            (
+                (ro_t, tab_i.at[0]), (rn_t, tab_i.at[1]), (go_t, tab_f.at[0]), (gn_t, tab_f.at[1]),
+                (rows_new.at[:, window], rz_new.at[mine, :]),
+                (rows_old.at[:, pl.ds(half, HALF)], rz_old.at[mine, :]),
+            )
         )
     ]
-    for load in loads:
-        load.start()
+    for copy in inputs:
+        copy.start()
 
     barrier = pltpu.get_barrier_semaphore()
     for r in range(15):
@@ -110,47 +119,29 @@
         pl.semaphore_signal(
             barrier, 1, device_id={"rep": lax.rem(rep + k, 8), "ep": ep}, device_id_type=MESH
         )
-    half = pl.multiple_of(core * HALF, 128)
-    other = pl.multiple_of((1 - core) * HALF, 128)
-    mine = pl.ds(pl.multiple_of(zl * ROWS, ROWS), ROWS)
+    loads = [
+        pltpu.make_async_copy(src, dst, ws.at[i])
+        for i, (src, dst) in enumerate(
+            ((w_new_hbm, w_raw.at[0]), (w_old_hbm, w_raw.at[1]), (w_out_hbm, w_out))
+        )
+    ]
+    for load in loads:
+        load.start()
+
     square[...] = jnp.zeros((128, 128), F32)
-    for i, table in enumerate((ro_t, rn_t, go_t, gn_t)):
+    for copy in inputs[:4]:
+        copy.wait()
+    for i, table in enumerate((tab_i.at[0], tab_i.at[1], tab_f.at[0], tab_f.at[1])):
         square[8 * i : 8 * i + 8, 0:ROWS] = table[...].astype(F32)
     meta_z[mine, :] = square[...].T[:ROWS, :]
-    rz_old[mine, :] = rows_old[:, pl.ds(half, HALF)]
-    rz_new[mine, :] = rows_new[:, pl.ds(pl.multiple_of(zh * 896 + core * 384, 128), WIN)]
-    pl.semaphore_wait(barrier, 26)
-
-    def z_copy(o, kind):
-        offset = ZOFF[o]
-        there = lax.rem(z + offset, 16) // 4
-        if kind == 0:
-            src, land = meta_z.at[mine, :], meta_z
-        elif kind == 1:
-            window = pl.ds(pl.multiple_of(there * 896 + core * 384, 128), WIN)
-            src, land = rows_new.at[:, window], rz_new
-        else:
-            src, land = rows_old.at[:, pl.ds(half, HALF)], rz_old
-        return remote(src, land.at[mine, :], zs.at[kind, o], zr.at[kind, o], z_dev(offset))
-
-    def z_from(o, kind, buf):
-        src = lax.rem(zl + 16 - ZOFF[o], 4)
-        ref = buf.at[pl.ds(pl.multiple_of(src * ROWS, ROWS), ROWS), :]
-        return remote(ref, ref, zs.at[kind, o], zr.at[kind, o], z_dev(ZOFF[o]))
-
-    for kind in range(3):
-        for o in range(3):
-            z_copy(o, kind).start()
-    for o in range(3):
-        z_from(o, 0, meta_z).wait_recv()
 
     lane = iota((4 * ROWS, 128), 1)
     p_row, p_col = iota((4 * ROWS, 4 * ROWS), 0), iota((4 * ROWS, 4 * ROWS), 1)
     before = jnp.where((p_col < p_row) & (p_col >> 5 == p_row >> 5), 1.0, 0.0).astype(BF)
     qs = iota((16 * SLOTS, 128), 0)
     rq = by24(qs)
-    dx = far(rq & 3)
-    dy = (far(rq >> 2) - dx) & 3
+    dx = far(rq >> 2)
+    dy = far(rq & 3)
     expert = (((x + dx) & 3) * 4 + ((y + dy) & 3)) * 4 + zl
     pick = jnp.where(expert == iota((16 * SLOTS, 128), 1), 1.0, 0.0).astype(BF)
     in_q = qs - by24(qs) * 24
@@ -160,7 +151,32 @@
     in_l = ql - by24(ql) * 24
     slot_l = (in_l - by6(in_l) * 6).astype(F32)
     same_l = by6(in_l) == iota((128, 16 * SLOTS), 0) >> 5
-    for b in range(2):
+    pl.semaphore_wait(barrier, 26)
+
+    def z_copy(o, kind):
+        offset = zoff[o]
+        there = lax.rem(z + offset, 16) // 4
+        if kind == 0:
+            src, land = meta_z.at[mine, :], meta_z
+        elif kind == 1:
+            theirs = pl.ds(pl.multiple_of(there * 896 + core * 384, 128), WIN)
+            src, land = rows_new.at[:, theirs], rz_new
+        else:
+            src, land = rows_old.at[:, pl.ds(half, HALF)], rz_old
+        return remote(src, land.at[mine, :], zs.at[kind, o], zr.at[kind, o], z_dev(offset))
+
+    def z_from(o, kind, buf):
+        src = lax.rem(zl + 16 - zoff[o], 4)
+        ref = buf.at[pl.ds(pl.multiple_of(src * ROWS, ROWS), ROWS), :]
+        return remote(ref, ref, zs.at[kind, o], zr.at[kind, o], z_dev(zoff[o]))
+
+    for kind in range(3):
+        for o in range(3):
+            z_copy(o, kind).start()
+    for o in range(3):
+        z_from(o, 0, meta_z).wait_recv()
+
+    def tables(b):
         named = jnp.zeros((4 * ROWS, 128), F32)
         gate = jnp.zeros((4 * ROWS, 128), F32)
         for k in range(TOPK):
@@ -188,21 +204,29 @@
         v = buf[4 * n : 4 * n + 4, h * SLOTS : (h + 1) * SLOTS, :]
         return v.astype(F32).reshape(CH, width).astype(BF)
 
-    def dispatch(b, rz, buf, land, width):
+    def send_out(b, buf, land, n):
+        for r in range(4 * n, 4 * n + 4):
+            if r < 15:
+                message(b, buf, land, r).start()
+            else:
+                land[15] = buf[15]
+
+    def dispatch(b, rz, buf, land, width, ahead):
         for n in range(4):
             put(buf, n, dot(disp[b, n * CH : (n + 1) * CH, :], rz[...]), width)
-            for r in range(4 * n, 4 * n + 4):
-                if r < 15:
-                    message(b, buf, land, r).start()
-                else:
-                    land[15] = buf[15]
-
+            if n < ahead:
+                send_out(b, buf, land, n)
+
+    tables(1)
     for o in range(3):
         z_from(o, 1, rz_new).wait_recv()
-    dispatch(1, rz_new, send_new, recv_new, WIN // 2)
+    inputs[4].wait()
+    dispatch(1, rz_new, send_new, recv_new, WIN // 2, 4)
+    tables(0)
     for o in range(3):
         z_from(o, 2, rz_old).wait_recv()
-    dispatch(0, rz_old, send_old, recv_old, BLK)
+    inputs[5].wait()
+    dispatch(0, rz_old, send_old, recv_old, BLK, 2)
 
     loads[0].wait()
     w_wide[...] = w_raw[0].astype(F32)
@@ -281,13 +305,16 @@
             else:
                 rb_recv[b, 15] = rb_send[b, 15]
 
-    for n in range(6):
+    for n in range(5):
         if n < 4:
             act_part(n)
-        if 1 <= n < 5:
+        if n >= 1:
             act_far(n - 1)
-        if n >= 2:
-            act_near(n - 2)
+
+    for n in range(2, 4):
+        for r in range(4 * n - 8, 4 * n - 4):
+            message(0, send_old, recv_old, r).wait_send()
+        send_out(0, send_old, recv_old, n)
 
     def fwd_copy(r):
         return remote(recv_old.at[r], sib_old.at[r], fs.at[r], fr.at[r], sibling)
@@ -319,6 +346,7 @@
     for n in range(6):
         if n < 4:
             forward(n)
+            act_near(n)
         if 1 <= n < 5:
             act_old(n - 1)
         if n >= 2:
@@ -333,22 +361,23 @@
             act += rn_recv[n, i].astype(F32)
         down(1, n, act)
 
-    for n in range(6):
+    for n in range(5):
         if n < 4:
             act_new(n)
         if 1 <= n < 5:
             chip_sum(1, n - 1)
             send_back(1, 0, n - 1)
-        if n >= 2:
-            send_back(1, 1, n - 2)
+
+    for n in range(4):
+        send_back(1, 1, n)
 
     def z1_copy(b, part, o):
-        at = pl.ds(pl.multiple_of(lax.rem(zl + ZOFF[o], 4) * ROWS, ROWS), ROWS)
+        at = pl.ds(pl.multiple_of(lax.rem(zl + zoff[o], 4) * ROWS, ROWS), ROWS)
         col, width = PARTS[part]
         cols = slice(col, col + 2 * width)
         return remote(
             z1_send.at[b, at, cols], z1_recv.at[b, o, :, cols],
-            z1s.at[b, part, o], z1r.at[b, part, o], z_dev(ZOFF[o]),
+            z1s.at[b, part, o], z1r.at[b, part, o], z_dev(zoff[o]),
         )
 
     def combine(b, part):
@@ -403,18 +432,22 @@
                 remote(ref, ref, z2s.at[b, 0], z2r.at[b, s], sibling).wait_recv()
 
         total = sum(z2_recv[b, s].astype(F32) for s in range(4))
-        out[...] = jnp.where(core == 0, total[:, :SLICE], total[:, WIN - SLICE :]).astype(BF)
+        result[b] = jnp.where(core == 0, total[:, :SLICE], total[:, WIN - SLICE :]).astype(BF)
+        pltpu.make_async_copy(result.at[b], out, ins.at[b]).start()
 
     combine(0, 0)
     combine(0, 1)
     spread(0, 0)
     spread(0, 1)
-    finish(0, out_old)
     combine(1, 0)
     spread(1, 0)
     combine(1, 1)
+    finish(0, out_old)
     spread(1, 1)
     finish(1, out_new)
+
+    for b, out in enumerate((out_old, out_new)):
+        pltpu.make_async_copy(result.at[b], out, ins.at[b]).wait()
 
     for o in range(3):
         for kind in range(3):
@@ -432,7 +465,8 @@
     for r in range(16):
         fwd_copy(r).wait_send()
     for r in range(15):
-        message(0, send_old, recv_old, r).wait_send()
+        if r >= 8:
+            message(0, send_old, recv_old, r).wait_send()
         message(1, send_new, recv_new, r).wait_send()
         for b in range(2):
             for part in range(2):
@@ -448,15 +482,18 @@
 def body(rows_old, rows_new, routes_old, routes_new, gates_old, gates_new, w_in_old, w_in_new, w_out):
     w_old = w_in_old[0].reshape(2 * D, SLAB)
     w_new = w_in_new[0].reshape(SLICE, 2, 8, SLAB).transpose(0, 2, 1, 3).reshape(SLICE * 16, SLAB)
-    vmem = pl.BlockSpec(memory_space=pltpu.VMEM)
+    hbm = pl.BlockSpec(memory_space=pl.ANY)
     dma = pltpu.SemaphoreType.DMA
     out = jax.ShapeDtypeStruct((ROWS, SLICE), BF)
     return pl.pallas_call(
         kernel,
         out_shape=(out, out),
-        in_specs=[vmem] * 6 + [pl.BlockSpec(memory_space=pl.ANY)] * 3,
-        out_specs=(vmem, vmem),
+        in_specs=[hbm] * 9,
+        out_specs=(hbm, hbm),
         scratch_shapes=[
+            pltpu.VMEM((2, TOPK, ROWS), jnp.int32),
+            pltpu.VMEM((2, TOPK, ROWS), F32),
+            pltpu.VMEM((2, ROWS, SLICE), BF),
             pltpu.VMEM((2, 2 * D, SLAB), BF),
             pltpu.VMEM((2 * D, SLAB), F32),
             pltpu.VMEM((D, 2 * SLAB), BF),
@@ -492,6 +529,7 @@
             pltpu.VMEM((2, 3, ROWS, HALF), BF),
             pltpu.VMEM((2, ROWS, HALF), BF),
             pltpu.VMEM((2, 4, ROWS, WIN), BF),
+            dma((6,)),
             dma((3,)),
             dma((3, 3)), dma((3, 3)),
             dma((2, 16)), dma((2, 16)),

time: 136 us -> 113 us (0.83)
  the two profiles are of different devices: /device:TPU:171 before, /device:TPU:5 now
where the time goes in v4:
time: 113 us
  Pallas kernels  109 us (96%)
  local copies, waits for them, and re-layouts  2.75 us (2%)
    pallas_call x1, Pallas kernels, body(): pl.pallas_call(kernel, out_shape=(out, out), in_specs=[hbm] * 9, out_spec...  109 us
    unnamed x2, local copies, waits for them, and re-layouts  2.75 us

profile of v4, /device:TPU:5, one launch (start us, length us, event | category | flops | bytes accessed | tf_op | source)
XLA Modules:
  0.0 112.7 jit_solution(1100232275868758547)
XLA Ops:
  0.6 109.3 %shard_map.104 = (bf16[32,448]{1,0:T(8,128)(2,1)}, bf16[32,448]{1,0:T(8,128)(2,1)}) custom-call(s32[8,32]{1,0:T(8,128)} %bitcast.14, s32[8,32]{1,0:T(8,128)} %bitcast.15, f32[8,32]{1,0:T(8,128)} %bitcast.16, f32[8,32]{1,0:T(8,128)} %bitcast.17, bf16[32,3584]{1,0:T(8,128)(2,1)} %rows_old.1, bf16[32,3584]{1,0:T(8,128)(2,1)} %rows_new.1, ...), custom_call_target="tpu_custom_call" | custom-call | tf_op jit(solution)/shard_map/pallas_call | solution.py:488
  110.0 1.4 %copy.14 = bf16[32,448]{1,0:T(8,128)(2,1)} copy(bf16[32,448]{1,0:T(8,128)(2,1)} %get-tuple-element.4) | data formatting | bytes 57344
  111.3 1.4 %copy.15 = bf16[32,448]{1,0:T(8,128)(2,1)} copy(bf16[32,448]{1,0:T(8,128)(2,1)} %get-tuple-element.5) | data formatting | bytes 57344

commit v5 on v4

--- a/solution.py
+++ b/solution.py
@@ -23,7 +23,7 @@
 SLOTS = 4 * CAP
 CH = 4 * SLOTS
 FAR = (2, 1, 3, 0)
-PLACE = tuple((dx, dy) for dx in FAR for dy in FAR)
+PLACE = tuple((dx, (total - dx) % 4) for total in FAR for dx in FAR)
 PART_A, PART_B = 512, 384
 PARTS = ((0, PART_A), (2 * PART_A, PART_B))
 
@@ -140,8 +140,8 @@
     before = jnp.where((p_col < p_row) & (p_col >> 5 == p_row >> 5), 1.0, 0.0).astype(BF)
     qs = iota((16 * SLOTS, 128), 0)
     rq = by24(qs)
-    dx = far(rq >> 2)
-    dy = far(rq & 3)
+    dx = far(rq & 3)
+    dy = (far(rq >> 2) - dx) & 3
     expert = (((x + dx) & 3) * 4 + ((y + dy) & 3)) * 4 + zl
     pick = jnp.where(expert == iota((16 * SLOTS, 128), 1), 1.0, 0.0).astype(BF)
     in_q = qs - by24(qs) * 24
@@ -193,7 +193,14 @@
         comb[b, 1] = jnp.where(chosen, dot_nt(low, pick), 0.0).astype(BF)
 
     def message(b, buf, land, r):
-        return remote(buf.at[r], land.at[r], xs.at[b, r], xr.at[b, r], to_dev(r))
+        return remote(buf.at[r], land.at[r], xs.at[b, r // 4], xr.at[b, r // 4], to_dev(r))
+
+    def others(n):
+        return slice(4 * n, min(4 * n + 4, 15))
+
+    def chunk(b, buf, land, n):
+        at = others(n)
+        return remote(buf.at[at], land.at[at], xs.at[b, n], xr.at[b, n], sibling)
 
     def put(buf, n, value, width):
         v = value.reshape(4, SLOTS, 2 * width)
@@ -248,8 +255,7 @@
         return remote(rn_send.at[n, i], rn_recv.at[n, i], rns.at[n, i], rnr.at[n, i], zh_dev(1 + 2 * i))
 
     def act_part(n):
-        for r in range(4 * n, min(4 * n + 4, 15)):
-            message(1, send_new, recv_new, r).wait_recv()
+        chunk(1, send_new, recv_new, n).wait_recv()
         rows = [take(recv_new, n, h, WIN // 2) for h in range(2)]
 
         def part(c):
@@ -288,7 +294,13 @@
 
     def back(b, part, r):
         src, land = ((ra_send, ra_recv), (rb_send, rb_recv))[part]
-        return remote(src.at[b, r], land.at[b, r], rts.at[b, part, r], rtr.at[b, part, r], from_dev(r))
+        n = r // 4
+        return remote(src.at[b, r], land.at[b, r], rts.at[b, part, n], rtr.at[b, part, n], from_dev(r))
+
+    def back_chunk(b, part, n):
+        src, land = ((ra_send, ra_recv), (rb_send, rb_recv))[part]
+        at = others(n)
+        return remote(src.at[b, at], land.at[b, at], rts.at[b, part, n], rtr.at[b, part, n], sibling)
 
     def chip_sum(b, n):
         so_copy(b, n).wait_recv()
@@ -312,26 +324,23 @@
             act_far(n - 1)
 
     for n in range(2, 4):
-        for r in range(4 * n - 8, 4 * n - 4):
-            message(0, send_old, recv_old, r).wait_send()
+        chunk(0, send_old, recv_old, n - 2).wait_send()
         send_out(0, send_old, recv_old, n)
 
-    def fwd_copy(r):
-        return remote(recv_old.at[r], sib_old.at[r], fs.at[r], fr.at[r], sibling)
+    def fwd_copy(n):
+        at = slice(4 * n, 4 * n + 4)
+        return remote(recv_old.at[at], sib_old.at[at], fs.at[n], fr.at[n], sibling)
 
     def forward(n):
-        for r in range(4 * n, 4 * n + 4):
-            if r < 15:
-                message(0, send_old, recv_old, r).wait_recv()
-            fwd_copy(r).start()
+        chunk(0, send_old, recv_old, n).wait_recv()
+        fwd_copy(n).start()
 
     def act_old(n):
         act = jnp.zeros((CH, 2 * SLAB), F32)
         for h in range(2):
             at = pl.ds(pl.multiple_of(half + h * BLK, 128), BLK)
             act += dot(take(recv_old, n, h, BLK), w_old[at, :])
-        for r in range(4 * n, 4 * n + 4):
-            fwd_copy(r).wait_recv()
+        fwd_copy(n).wait_recv()
         for h in range(2):
             at = pl.ds(pl.multiple_of(other + h * BLK, 128), BLK)
             act += dot(take(sib_old, n, h, BLK), w_old[at, :])
@@ -381,8 +390,8 @@
         )
 
     def combine(b, part):
-        for r in range(15):
-            back(b, part, r).wait_recv()
+        for n in range(4):
+            back_chunk(b, part, n).wait_recv()
         col, width = PARTS[part]
         for h in range(2):
             rows = (ra_recv, rb_recv)[part][b, :, h * SLOTS : (h + 1) * SLOTS, :]
@@ -462,15 +471,14 @@
             rn_copy(n, i).wait_send()
         for b in range(2):
             so_copy(b, n).wait_send()
-    for r in range(16):
-        fwd_copy(r).wait_send()
-    for r in range(15):
-        if r >= 8:
-            message(0, send_old, recv_old, r).wait_send()
-        message(1, send_new, recv_new, r).wait_send()
+    for n in range(4):
+        fwd_copy(n).wait_send()
+        if n >= 2:
+            chunk(0, send_old, recv_old, n).wait_send()
+        chunk(1, send_new, recv_new, n).wait_send()
         for b in range(2):
             for part in range(2):
-                back(b, part, r).wait_send()
+                back_chunk(b, part, n).wait_send()
     for b in range(2):
         for t in range(4):
 
@@ -532,13 +540,13 @@
             dma((6,)),
             dma((3,)),
             dma((3, 3)), dma((3, 3)),
-            dma((2, 16)), dma((2, 16)),
-            dma((16,)), dma((16,)),
+            dma((2, 4)), dma((2, 4)),
+            dma((4,)), dma((4,)),
             dma((4,)), dma((4,)),
             dma((4, 2)), dma((4, 2)),
             dma((4, 2)), dma((4, 2)),
             dma((2, 4)), dma((2, 4)),
-            dma((2, 2, 16)), dma((2, 2, 16)),
+            dma((2, 2, 4)), dma((2, 2, 4)),
             dma((2, 2, 3)), dma((2, 2, 3)),
             dma((2, 4)), dma((2, 4)),
         ],

time: 113 us -> 105 us (0.929)
  the two profiles are of different devices: /device:TPU:5 before, /device:TPU:163 now
where the time goes in v5:
time: 105 us
  Pallas kernels  101 us (96%)
  local copies, waits for them, and re-layouts  2.75 us (3%)
    pallas_call x1, Pallas kernels, body(): pl.pallas_call(kernel, out_shape=(out, out), in_specs=[hbm] * 9, out_spec...  101 us
    unnamed x2, local copies, waits for them, and re-layouts  2.75 us

profile of v5, /device:TPU:163, one launch (start us, length us, event | category | flops | bytes accessed | tf_op | source)
XLA Modules:
  0.0 104.7 jit_solution(40736518555841506)
XLA Ops:
  0.6 101.3 %shard_map.104 = (bf16[32,448]{1,0:T(8,128)(2,1)}, bf16[32,448]{1,0:T(8,128)(2,1)}) custom-call(s32[8,32]{1,0:T(8,128)} %bitcast.14, s32[8,32]{1,0:T(8,128)} %bitcast.15, f32[8,32]{1,0:T(8,128)} %bitcast.16, f32[8,32]{1,0:T(8,128)} %bitcast.17, bf16[32,3584]{1,0:T(8,128)(2,1)} %rows_old.1, bf16[32,3584]{1,0:T(8,128)(2,1)} %rows_new.1, ...), custom_call_target="tpu_custom_call" | custom-call | tf_op jit(solution)/shard_map/pallas_call | solution.py:496
  102.0 1.4 %copy.14 = bf16[32,448]{1,0:T(8,128)(2,1)} copy(bf16[32,448]{1,0:T(8,128)(2,1)} %get-tuple-element.4) | data formatting | bytes 57344
  103.4 1.4 %copy.15 = bf16[32,448]{1,0:T(8,128)(2,1)} copy(bf16[32,448]{1,0:T(8,128)(2,1)} %get-tuple-element.5) | data formatting | bytes 57344

commit v6 on v5

--- a/solution.py
+++ b/solution.py
@@ -171,7 +171,7 @@
         return remote(ref, ref, zs.at[kind, o], zr.at[kind, o], z_dev(zoff[o]))
 
     for kind in range(3):
-        for o in range(3):
+        for o in (2, 0, 1):
             z_copy(o, kind).start()
     for o in range(3):
         z_from(o, 0, meta_z).wait_recv()
@@ -294,13 +294,11 @@
 
     def back(b, part, r):
         src, land = ((ra_send, ra_recv), (rb_send, rb_recv))[part]
-        n = r // 4
-        return remote(src.at[b, r], land.at[b, r], rts.at[b, part, n], rtr.at[b, part, n], from_dev(r))
-
-    def back_chunk(b, part, n):
+        return remote(src.at[b, r], land.at[b, r], rts.at[b, part], rtr.at[b, part], from_dev(r))
+
+    def back_all(b, part):
         src, land = ((ra_send, ra_recv), (rb_send, rb_recv))[part]
-        at = others(n)
-        return remote(src.at[b, at], land.at[b, at], rts.at[b, part, n], rtr.at[b, part, n], sibling)
+        return remote(src.at[b, 0:15], land.at[b, 0:15], rts.at[b, part], rtr.at[b, part], sibling)
 
     def chip_sum(b, n):
         so_copy(b, n).wait_recv()
@@ -390,8 +388,7 @@
         )
 
     def combine(b, part):
-        for n in range(4):
-            back_chunk(b, part, n).wait_recv()
+        back_all(b, part).wait_recv()
         col, width = PARTS[part]
         for h in range(2):
             rows = (ra_recv, rb_recv)[part][b, :, h * SLOTS : (h + 1) * SLOTS, :]
@@ -400,7 +397,7 @@
             cols = slice(col + h * width, col + (h + 1) * width)
             z1_own[b, :, cols] = total
             z1_send[b, :, cols] = total.astype(BF)
-        for o in range(3):
+        for o in (2, 0, 1):
             z1_copy(b, part, o).start()
 
     def z2_copy(b, t):
@@ -441,7 +438,7 @@
                 remote(ref, ref, z2s.at[b, 0], z2r.at[b, s], sibling).wait_recv()
 
         total = sum(z2_recv[b, s].astype(F32) for s in range(4))
-        result[b] = jnp.where(core == 0, total[:, :SLICE], total[:, WIN - SLICE :]).astype(BF)
+        result[b] = jnp.where(core == 0, total[:, :SLICE], total[:, WIN - SLICE :])
         pltpu.make_async_copy(result.at[b], out, ins.at[b]).start()
 
     combine(0, 0)
@@ -449,10 +446,10 @@
     spread(0, 0)
     spread(0, 1)
     combine(1, 0)
+    combine(1, 1)
     spread(1, 0)
-    combine(1, 1)
+    spread(1, 1)
     finish(0, out_old)
-    spread(1, 1)
     finish(1, out_new)
 
     for b, out in enumerate((out_old, out_new)):
@@ -471,14 +468,14 @@
             rn_copy(n, i).wait_send()
         for b in range(2):
             so_copy(b, n).wait_send()
+    for b in range(2):
+        for part in range(2):
+            back_all(b, part).wait_send()
     for n in range(4):
         fwd_copy(n).wait_send()
         if n >= 2:
             chunk(0, send_old, recv_old, n).wait_send()
         chunk(1, send_new, recv_new, n).wait_send()
-        for b in range(2):
-            for part in range(2):
-                back_chunk(b, part, n).wait_send()
     for b in range(2):
         for t in range(4):
 
@@ -492,8 +489,8 @@
     w_new = w_in_new[0].reshape(SLICE, 2, 8, SLAB).transpose(0, 2, 1, 3).reshape(SLICE * 16, SLAB)
     hbm = pl.BlockSpec(memory_space=pl.ANY)
     dma = pltpu.SemaphoreType.DMA
-    out = jax.ShapeDtypeStruct((ROWS, SLICE), BF)
-    return pl.pallas_call(
+    out = jax.ShapeDtypeStruct((ROWS, SLICE), F32)
+    old, new = pl.pallas_call(
         kernel,
         out_shape=(out, out),
         in_specs=[hbm] * 9,
@@ -501,7 +498,7 @@
         scratch_shapes=[
             pltpu.VMEM((2, TOPK, ROWS), jnp.int32),
             pltpu.VMEM((2, TOPK, ROWS), F32),
-            pltpu.VMEM((2, ROWS, SLICE), BF),
+            pltpu.VMEM((2, ROWS, SLICE), F32),
             pltpu.VMEM((2, 2 * D, SLAB), BF),
             pltpu.VMEM((2 * D, SLAB), F32),
             pltpu.VMEM((D, 2 * SLAB), BF),
@@ -546,7 +543,7 @@
             dma((4, 2)), dma((4, 2)),
             dma((4, 2)), dma((4, 2)),
             dma((2, 4)), dma((2, 4)),
-            dma((2, 2, 4)), dma((2, 2, 4)),
+            dma((2, 2)), dma((2, 2)),
             dma((2, 2, 3)), dma((2, 2, 3)),
             dma((2, 4)), dma((2, 4)),
         ],
@@ -554,6 +551,7 @@
             collective_id=0, has_side_effects=True, vmem_limit_bytes=60 * 1024 * 1024
         ),
     )(routes_old.T, routes_new.T, gates_old.T, gates_new.T, rows_old, rows_new, w_old, w_new, w_out[0])
+    return old.astype(BF), new.astype(BF)
 
 
 def solution(mesh):

time: 105 us -> 98.6 us (0.939)
  the two profiles are of different devices: /device:TPU:163 before, /device:TPU:11 now
where the time goes in v6:
time: 98.6 us; the launch traced here: 98.3 us
  Pallas kernels  94.8 us (96%)
  other arithmetic  2.92 us (3%)
    pallas_call x1, Pallas kernels, body(): pl.pallas_call(kernel, out_shape=(out, out), in_specs=[hbm] * 9, out_spec...  94.8 us
    convert_element_type x2, other arithmetic, body(): return (old.astype(BF), new.astype(BF))  2.92 us

profile of v6, /device:TPU:11, one launch (start us, length us, event | category | flops | bytes accessed | tf_op | source)
XLA Modules:
  0.0 98.3 jit_solution(5437273006231771778)
XLA Ops:
  0.6 94.8 %shard_map.104 = (f32[32,448]{1,0:T(8,128)}, f32[32,448]{1,0:T(8,128)}) custom-call(s32[8,32]{1,0:T(8,128)} %bitcast.14, s32[8,32]{1,0:T(8,128)} %bitcast.15, f32[8,32]{1,0:T(8,128)} %bitcast.16, f32[8,32]{1,0:T(8,128)} %bitcast.17, bf16[32,3584]{1,0:T(8,128)(2,1)} %rows_old.1, bf16[32,3584]{1,0:T(8,128)(2,1)} %rows_new.1, bf16[7168,128]{1,0:T(8,128)(2,1)} %bitcast.11, ...), custom_call_target="tpu_custom_call" | custom-call | tf_op jit(solution)/shard_map/pallas_call | solution.py:493
  95.4 1.5 %convert_element_type.6 = bf16[32,448]{1,0:T(8,128)(2,1)} convert(f32[32,448]{1,0:T(8,128)} %get-tuple-element.4) | non-fusion elementwise | flops 14336 | bytes 86016 | tf_op jit(solution)/shard_map/convert_element_type | solution.py:554
  96.9 1.5 %convert_element_type.7 = bf16[32,448]{1,0:T(8,128)(2,1)} convert(f32[32,448]{1,0:T(8,128)} %get-tuple-element.5) | non-fusion elementwise | flops 14336 | bytes 86016 | tf_op jit(solution)/shard_map/convert_element_type | solution.py:554
